TPU v7x, 768 devices: a whole 4x8x12 slice. The times are simulated.
768 devices in a mesh: blk: 32 (over y, z_hi), rep: 24 (over x, z_lo, core).
Axes of the slice: x: 4, y: 8, z: 12 (z_hi: 4, z_lo: 3; z = z_hi * 3 + z_lo), core: 2. Of those that a mesh axis runs over, the one named last changes fastest.
Arguments:
- tokens: bfloat16 [98304, 8192], P(('blk', 'rep')), may hold values from -6 to 6
- gate_weight: bfloat16 [32, 8192], P('blk'), may hold values from -0.0625 to 0.0625
- up_weight: bfloat16 [32, 8192], P('blk'), may hold values from -0.0625 to 0.0625
- down_weight: bfloat16 [32, 8192], P('blk'), may hold values from -1 to 1
Outputs:
- grad_gate: float32 [32, 8192], P('blk')
- grad_up: float32 [32, 8192], P('blk')
- grad_down: float32 [32, 8192], P('blk')
All inputs are finite; a program needn't handle non-finite values.
Results may differ from a plain program's by a relative error of at most 0.0027.
Values may be sent and summed in bfloat16 or wider, within the bound.
No kernel may reach another device: no remote copies, remote signals or barrier semaphores. Data moves between devices by JAX's collectives and lax.ppermute only.
A program may use at most 32 MiB of HBM per device.

v0:
```python
import jax
import jax.numpy as jnp
from jax import lax
from jax.sharding import Mesh
from jax.sharding import PartitionSpec as P

BLK = ("blk_0", "blk_1")
BLK_REP = ("blk_0", "blk_1", "rep")


def side_by_side(arrays, axis, dim, along):
    ends, at = ([], 0)
    for a in arrays[:-1]:
        at += a.shape[along]
        ends.append(at)
    both = jnp.concatenate(arrays, axis=along)
    return tuple(jnp.split(lax.all_gather(both, axis, axis=dim, tiled=True), ends, axis=along))


def own_rows(total, axes):
    for axis in axes:
        total = lax.psum_scatter(total, axis, scatter_dimension=0, tiled=True)
    return total


def sent_to_all(x, axis):
    peers = lax.axis_size(axis)
    return lax.all_to_all(jnp.broadcast_to(x[None], (peers, *x.shape)), axis, 0, 0, tiled=True)


def over_copies(x, axis):
    return sent_to_all(x, axis).sum(axis=0)


def per_device(tokens, gate_weight, up_weight, down_weight):
    tok_rows = tokens.shape[0]
    features = tokens.shape[1]
    cycle_size = lax.axis_size(BLK)
    group_size = lax.axis_size("rep")
    loss_scale = float(tok_rows * cycle_size * group_size) ** (-0.5)
    right_numbers = (((1,), (1,)), ((), ()))
    left_numbers = (((0,), (0,)), ((), ()))
    gate_piece, up_piece, down_piece = side_by_side(
        (gate_weight, up_weight, down_weight), BLK, 0, 1
    )
    gate_pre = lax.dot_general(
        tokens, gate_piece, right_numbers, preferred_element_type=jnp.float32
    )
    up_pre = lax.dot_general(tokens, up_piece, right_numbers, preferred_element_type=jnp.float32)
    hidden_piece = (gate_pre * jax.nn.sigmoid(gate_pre) * up_pre).astype(jnp.bfloat16)
    layer_out = jnp.dot(hidden_piece, down_piece, preferred_element_type=jnp.float32)
    gate_all = gate_pre
    up_all = up_pre
    gate_full = gate_piece
    up_full = up_piece
    down_full = down_piece
    carry = (layer_out, gate_all, up_all, hidden_piece, gate_full, up_full, down_full)
    layer_out, gate_pre, up_pre, hidden, gate_full, up_full, down_full = carry
    cotangent = (layer_out * loss_scale).astype(jnp.bfloat16)
    hidden_grad = lax.dot_general(
        cotangent, down_full, right_numbers, preferred_element_type=jnp.float32
    )
    sigmoid_gate = jax.nn.sigmoid(gate_pre)
    active = gate_pre * sigmoid_gate
    gate_grad = (
        hidden_grad * up_pre * (sigmoid_gate * (1.0 + gate_pre * (1.0 - sigmoid_gate)))
    ).astype(jnp.bfloat16)
    up_grad = (hidden_grad * active).astype(jnp.bfloat16)
    gate_term = lax.dot_general(gate_grad, tokens, left_numbers, preferred_element_type=jnp.float32)
    up_term = lax.dot_general(up_grad, tokens, left_numbers, preferred_element_type=jnp.float32)
    down_term = lax.dot_general(hidden, cotangent, left_numbers, preferred_element_type=jnp.float32)
    shares = own_rows(jnp.concatenate([gate_term, up_term, down_term], axis=1), BLK)
    totals = over_copies(shares, "rep")
    return (totals[:, :features], totals[:, features : 2 * features], totals[:, 2 * features :])


def solution(mesh):
    split = Mesh(mesh.devices.reshape(8, 4, mesh.shape["rep"]), ("blk_0", "blk_1", "rep"))
    return jax.shard_map(
        per_device,
        mesh=split,
        in_specs=(P(BLK_REP, None), P(BLK, None), P(BLK, None), P(BLK, None)),
        out_specs=(P(BLK, None), P(BLK, None), P(BLK, None)),
        check_vma=False,
    )
```

profile of v0, /device:TPU:1, one launch (start us, length us, event | category | flops | bytes accessed | tf_op | source)
XLA Modules:
  0.0 374.4 jit_solution(750206051630544965)
XLA Ops:
  7.2 0.0 copy-start
  7.2 0.0 all-gather.3.cloned.1.call-start
  7.2 1.7 maximum_bitcast_fusion
  8.9 0.0 all-gather.3.cloned.1.call-update
  8.9 0.0 all-reduce.5.cloned.1.call-start
  9.0 122.3 %all-gather.3.cloned.1.call-done = bf16[32,1,24576]{2,1,0:T(2,128)(2,1)} async-done(((bf16[1,1,24576]{2,1,0:T(2,128)(2,1)}), bf16[32,1,24576]{2,1,0:T(2,128)(2,1)}) %all-gather.3.cloned.1.call-update) | async-done | bytes 1572880 | tf_op jit(solution)/shard_map/all_gather | solution.py:17
  131.3 3.6 copy.11
  134.9 0.0 copy-done
  134.9 0.8 convolution_bitcast_fusion.1
  135.7 0.8 multiply_convert_fusion.2
  136.5 0.7 fusion
  137.3 0.8 fusion.3
  138.1 0.4 fusion.14
  138.5 0.4 fusion.8
  138.9 0.4 fusion.7
  139.3 1.9 pad_maximum_fusion
  141.2 0.0 all-reduce.5.cloned.1.call-update
  141.2 0.0 all-reduce.7.cloned.1.call-start
  141.3 1.3 dynamic-slice
  143.2 97.5 %all-reduce.5.cloned.1.call-done = f32[32,24576]{1,0:T(8,128)} async-done(((f32[32,24576]{1,0:T(8,128)}), f32[32,24576]{1,0:T(8,128)}) %all-reduce.5.cloned.1.call-update) | async-done | bytes 3145744
  240.7 2.0 constant_dynamic-slice_fusion.1
  242.7 0.0 all-reduce.7.cloned.1.call-update
  242.7 1.3 dynamic-slice.2
  244.0 70.2 %all-reduce.7.cloned.1.call-done = f32[4,24576]{1,0:T(4,128)} async-done(((f32[4,24576]{1,0:T(4,128)}), f32[4,24576]{1,0:T(4,128)}) %all-reduce.7.cloned.1.call-update) | async-done | bytes 393232
  314.2 1.7 constant_dynamic-slice_fusion
  315.9 2.0 broadcast_in_dim.9
  317.9 46.1 %all_to_all.5 = f32[24,1,24576]{2,1,0:T(1,128)} all-to-all(f32[24,1,24576]{2,1,0:T(1,128)S(1)} %broadcast_in_dim.9), channel_id=1, replica_groups=mesh['blk_0'=8,'blk_1'=4,'rep'=24] {'rep'}, dimensions={0} | all-to-all | bytes 4718592 | tf_op jit(solution)/shard_map/all_to_all | solution.py:28
  364.0 3.2 reduce_sum.11
  367.2 0.6 fusion.13
Async XLA Ops:
  7.2 127.7 %copy-start = (bf16[128,8192]{1,0:T(8,128)(2,1)S(1)}, bf16[128,8192]{1,0:T(8,128)(2,1)}, u32[]{:S(2)}) copy-start(bf16[128,8192]{1,0:T(8,128)(2,1)} %param.4) | copy-start | bytes 6291460
  7.2 124.1 %all-gather.3.cloned.1.call-start = ((), (), s32[]{:S(2)}) async-start(), calls=%async_computation.1 | async-start | bytes 3244032 | tf_op jit(solution)/shard_map/all_gather | solution.py:17
  8.9 231.8 %all-reduce.5.cloned.1.call-start = ((), (), s32[]{:S(2)}) async-start(), calls=%async_computation.2 | async-start | bytes 6291456
  141.2 172.9 %all-reduce.7.cloned.1.call-start = ((), (), s32[]{:S(2)}) async-start(), calls=%async_computation.3 | async-start | bytes 786432
Sparse Core Ops, SparseCore 0:
  11.8 119.4 all-gather.2
  141.4 99.3 all-reduce.4
  244.0 70.1 all-reduce.6
where the time goes:
time: 375 us; the launch traced here: 374 us
  waiting for transfers between devices  290 us (77%)
  blocking collectives  46.1 us (12%)
  between operations  14.4 us (4%)
  local copies, waits for them, and re-layouts  12.5 us (3%)
  other arithmetic  6.74 us (2%)
  matrix products  4.44 us (1%)
    unnamed x5, waiting for transfers between devices  168 us
    all_gather x1, waiting for transfers between devices, side_by_side(): lax.all_gather(both, axis, axis=dim, tiled=True)  122 us
    all_to_all x1, blocking collectives, sent_to_all(): lax.all_to_all(jnp.broadcast_to(x[None], (peers, *x.shape)), axis, 0, 0,...  46.1 us
    unnamed x7, local copies, waits for them, and re-layouts  9.85 us
  transfers between devices with their start and end apart: 3, of which 3 were waited for; matrix products, arithmetic and copies ran while one was open for 1% of the time, Pallas kernels for 0%

commit v1 on v0

v1 whole, which is shorter than its diff:
```python
import jax
import jax.numpy as jnp
from jax import lax
from jax.experimental import pallas as pl
from jax.experimental.pallas import tpu as pltpu
from jax.sharding import Mesh
from jax.sharding import PartitionSpec as P

BLK = ("y", "zh")
Z = ("zh", "zl")
REP = ("x", "zl", "c")
NT = (((1,), (1,)), ((), ()))


def sent_to_all(x, axis):
    peers = lax.axis_size(axis)
    return lax.all_to_all(jnp.broadcast_to(x[None], (peers, *x.shape)), axis, 0, 0, tiled=True)


def layer_kernel(loss_scale, core_ref, tok_ref, own_ref, oth_ref, keep_ref, send_ref, cot_ref):
    parts, rows, width = own_ref.shape
    hid = rows // 3
    half = parts * width
    core = core_ref[0]

    def columns(which, part):
        side = core if which == 0 else 1 - core
        return pl.ds(pl.multiple_of(side * half + part * width, width), width)

    pieces = [(which, part) for which in range(2) for part in range(parts)]
    held = (own_ref, oth_ref)
    out = (keep_ref, send_ref)
    pre = jnp.zeros((tok_ref.shape[0], 2 * hid), jnp.float32)
    for which, part in pieces:
        pre += lax.dot_general(
            tok_ref[:, columns(which, part)],
            held[which][part, : 2 * hid, :],
            NT,
            preferred_element_type=jnp.float32,
        )
    gate_pre = pre[:, :hid]
    up_pre = pre[:, hid:]
    sigmoid_gate = jax.nn.sigmoid(gate_pre)
    active = gate_pre * sigmoid_gate
    hidden_wide = (active * up_pre).astype(jnp.bfloat16).astype(jnp.float32)
    hidden = hidden_wide.astype(jnp.bfloat16)
    hidden_t = hidden_wide.T.astype(jnp.bfloat16)
    hidden_grad = jnp.zeros(gate_pre.shape, jnp.float32)
    for which, part in pieces:
        down = held[which][part, 2 * hid :, :]
        layer_out = jnp.dot(hidden, down, preferred_element_type=jnp.float32)
        cotangent = (layer_out * loss_scale).astype(jnp.bfloat16)
        cot_ref[which * parts + part] = cotangent
        hidden_grad += lax.dot_general(cotangent, down, NT, preferred_element_type=jnp.float32)
    gate_grad = hidden_grad * up_pre * (sigmoid_gate * (1.0 + gate_pre * (1.0 - sigmoid_gate)))
    up_grad = hidden_grad * active
    grads_t = jnp.concatenate([gate_grad, up_grad], axis=1).T.astype(jnp.bfloat16)
    for which, part in pieces[parts:] + pieces[:parts]:
        out[which][part, : 2 * hid, :] = jnp.dot(
            grads_t, tok_ref[:, columns(which, part)], preferred_element_type=jnp.float32
        )
        out[which][part, 2 * hid :, :] = jnp.dot(
            hidden_t, cot_ref[which * parts + part], preferred_element_type=jnp.float32
        )


def per_device(tokens, gate_weight, up_weight, down_weight):
    ys, zhs, xs, zls, cs = (lax.axis_size(a) for a in ("y", "zh", "x", "zl", "c"))
    tok_rows, features = tokens.shape
    devices = ys * zhs * xs * zls * cs
    loss_scale = float(tok_rows * devices) ** (-0.5)
    width = features // (xs * cs)
    rows = 3 * ys * zhs
    core = lax.axis_index("c")
    swap = [(i, (i + 1) % cs) for i in range(cs)]

    at = (core * xs + lax.axis_index("x")) * width
    mine = lax.select_n(lax.axis_index("zl"), gate_weight, up_weight, down_weight)
    piece = lax.dynamic_slice(mine, (0, at), (1, width))
    over_z = sent_to_all(piece[0], Z)
    over_y = sent_to_all(over_z, "y").reshape(ys, zhs, zls, width)
    plane = over_y.transpose(2, 0, 1, 3).reshape(rows, width)
    own = sent_to_all(plane, "x")
    other = lax.ppermute(own, "c", swap)

    vmem = pl.BlockSpec(memory_space=pltpu.VMEM)
    term = jax.ShapeDtypeStruct(own.shape, jnp.float32)
    keep, send = pl.pallas_call(
        lambda *refs: layer_kernel(loss_scale, *refs),
        out_shape=(term, term),
        in_specs=[pl.BlockSpec(memory_space=pltpu.SMEM), vmem, vmem, vmem],
        out_specs=(vmem, vmem),
        scratch_shapes=[pltpu.VMEM((cs * xs, tok_rows, width), jnp.bfloat16)],
        compiler_params=pltpu.CompilerParams(vmem_limit_bytes=32 << 20),
        name="layer",
    )(core.reshape(1), tokens, own, other)

    both = (keep + lax.ppermute(send, "c", swap)).astype(jnp.bfloat16)
    got = lax.all_to_all(both, "x", 0, 0, tiled=True)
    sum_x = got.astype(jnp.float32).sum(axis=0).astype(jnp.bfloat16)
    by_y = sum_x.reshape(zls, ys, zhs, width).transpose(1, 2, 0, 3).reshape(ys, zhs * zls, width)
    got = lax.all_to_all(by_y, "y", 0, 0, tiled=True)
    sum_y = got.astype(jnp.float32).sum(axis=0)
    got = lax.all_to_all(sum_y, Z, 0, 0, tiled=True)
    total = got.sum(axis=0)
    every = sent_to_all(total, REP).reshape(xs, zls, cs, width)
    result = every.transpose(1, 2, 0, 3).reshape(zls, 1, features)
    return (result[0], result[1], result[2])


def solution(mesh):
    shape = (8, 4, 4, 3, 2)
    split = Mesh(mesh.devices.reshape(shape), ("y", "zh", "x", "zl", "c"))
    return jax.shard_map(
        per_device,
        mesh=split,
        in_specs=(P(BLK + REP, None), P(BLK, None), P(BLK, None), P(BLK, None)),
        out_specs=(P(BLK, None), P(BLK, None), P(BLK, None)),
        check_vma=False,
    )
```

time: 375 us -> 131 us (0.35)
  waiting for transfers between devices: 290 us -> 4.9 us
  blocking collectives: 46.1 us -> 106 us
  between operations: 14.4 us -> 0.81 us
  local copies, waits for them, and re-layouts: 12.5 us -> 3.48 us
  starting transfers between devices: 0.12 us -> 9.04 us
  matrix products: 4.44 us -> 0 us
  other arithmetic: 6.74 us -> 2.32 us
  Pallas kernels: 0 us -> 4.02 us
    unnamed x5 -> x0, waiting for transfers between devices: 168 us -> none
    all_gather x1 -> x0, waiting for transfers between devices: 122 us -> none  [side_by_side(): lax.all_gather(both, axis, axis=dim, tiled=True)]
    all_to_all x0 -> x3, blocking collectives: none -> 39 us  [the longest x1 14.4 us: per_device(): got = lax.all_to_all(both, 'x', 0, 0, tiled=True)]
    all_to_all x1 -> x4, blocking collectives: 46.1 us -> 67.1 us  [sent_to_all(): lax.all_to_all(jnp.broadcast_to(x[None], (peers, *x.shape)), axis, 0, 0,...]
    unnamed x7 -> x5, local copies, waits for them, and re-layouts: 9.85 us -> 0.06 us
    ppermute x0 -> x2, starting transfers between devices: none -> 9.04 us  [the longest x1 6.77 us: per_device(): other = lax.ppermute(own, 'c', swap)]
    ppermute x0 -> x2, waiting for transfers between devices: none -> 4.9 us  [the longest x1 3.01 us: per_device(): both = (keep + lax.ppermute(send, 'c', swap)).astype(jnp.bfloat16)]
    dot_general x7 -> x0, matrix products: 4.44 us -> none  [the longest x1 0.83 us: per_device(): lax.dot_general(tokens, up_piece, right_numbers, preferred_element_type=j...]
  transfers between devices with their start and end apart: 3 -> 2, of which waited for: 3 -> 2; matrix products, arithmetic and copies ran while one was open for 1% -> 0% of each run, Pallas kernels for 0% -> 0%
where the time goes in v1:
time: 131 us
  blocking collectives  106 us (81%)
  starting transfers between devices  9.04 us (7%)
  waiting for transfers between devices  4.9 us (4%)
  Pallas kernels  4.02 us (3%)
  local copies, waits for them, and re-layouts  3.48 us (3%)
  other arithmetic  2.32 us (2%)
    all_to_all x4, blocking collectives, sent_to_all(): lax.all_to_all(jnp.broadcast_to(x[None], (peers, *x.shape)), axis, 0, 0,...  67.1 us
    all_to_all x1, blocking collectives, per_device(): got = lax.all_to_all(both, 'x', 0, 0, tiled=True)  14.4 us
    all_to_all x1, blocking collectives, per_device(): got = lax.all_to_all(by_y, 'y', 0, 0, tiled=True)  12.5 us
    all_to_all x1, blocking collectives, per_device(): got = lax.all_to_all(sum_y, Z, 0, 0, tiled=True)  12 us
    ppermute x1, starting transfers between devices, per_device(): other = lax.ppermute(own, 'c', swap)  6.77 us
    pallas_call x1, Pallas kernels, per_device(): pl.pallas_call(lambda *refs: layer_kernel(loss_scale, *refs), out_shape=(...  4.02 us
    ppermute x1, waiting for transfers between devices, per_device(): both = (keep + lax.ppermute(send, 'c', swap)).astype(jnp.bfloat16)  3.01 us
  transfers between devices with their start and end apart: 2, of which 2 were waited for; matrix products, arithmetic and copies ran while one was open for 0% of the time, Pallas kernels for 0%

profile of v1, /device:TPU:1, one launch (start us, length us, event | category | flops | bytes accessed | tf_op | source)
XLA Modules:
  0.0 130.7 jit_solution(16969186157356375499)
XLA Ops:
  0.7 0.8 fusion
  1.4 0.5 broadcast.9
  2.0 0.8 reduce.5
  2.8 24.8 %all_to_all.41 = bf16[12,2,512]{2,1,0:T(2,128)(2,1)S(1)} all-to-all(bf16[12,2,512]{2,1,0:T(2,128)(2,1)S(1)} %reshape.53), channel_id=1, replica_groups=mesh['y'=8,'zh'=4,'x'=4,'zl'=3,'c'=2] {'zh','zl'}, dimensions={0} | all-to-all | bytes 49152 | tf_op jit(solution)/shard_map/all_to_all | solution.py:17
  27.6 16.1 %all_to_all.42 = bf16[8,12,1024]{2,1,0:T(8,128)(2,1)S(1)} all-to-all(bf16[8,12,1024]{2,1,0:T(8,128)(2,1)S(1)} %broadcast_in_dim.28), channel_id=1, replica_groups=mesh['y'=8,'zh'=4,'x'=4,'zl'=3,'c'=2] {'y'}, dimensions={0} | all-to-all | bytes 393216 | tf_op jit(solution)/shard_map/all_to_all | solution.py:17
  43.7 0.1 copy.12
  43.8 0.2 copy.13
  44.0 0.0 copy-start
  44.0 0.1 broadcast_in_dim.29
  44.0 0.1 broadcast_in_dim.30
  44.1 12.3 %all_to_all.43.refs_2_ = bf16[4,96,1024]{2,1,0:T(8,128)(2,1)S(1)} all-to-all(bf16[4,96,1024]{2,1,0:T(8,128)(2,1)S(1)} %broadcast_in_dim.30), channel_id=1, replica_groups=mesh['y'=8,'zh'=4,'x'=4,'zl'=3,'c'=2] {'x'}, dimensions={0} | all-to-all | bytes 1572864 | tf_op jit(solution)/shard_map/all_to_all | solution.py:17
  56.4 6.8 %collective-permute-start = (bf16[4,96,1024]{2,1,0:T(8,128)(2,1)S(1)}, bf16[4,96,1024]{2,1,0:T(8,128)(2,1)S(1)}, u32[]{:S(2)}, u32[]{:S(2)}) collective-permute-start(bf16[4,96,1024]{2,1,0:T(8,128)(2,1)S(1)} %all_to_all.43.refs_2_), channel_id=1, source_target_pairs={{0,1},{1,0},{2,3},{3,2},{4,5},{5,4},{6,7},{7,6},{8,9},{9,8},{10,11... | collective-permute-start | bytes 2359304 | tf_op jit(solution)/shard_map/ppermute | solution.py:84
  63.2 1.9 %collective-permute-done.refs_3_ = bf16[4,96,1024]{2,1,0:T(8,128)(2,1)S(1)} collective-permute-done((bf16[4,96,1024]{2,1,0:T(8,128)(2,1)S(1)}, bf16[4,96,1024]{2,1,0:T(8,128)(2,1)S(1)}, u32[]{:S(2)}, u32[]{:S(2)}) %collective-permute-start) | collective-permute-done | bytes 786464 | tf_op jit(solution)/shard_map/ppermute | solution.py:84
  65.1 0.0 copy-done
  65.1 4.0 %layer.1 = (f32[4,96,1024]{2,1,0:T(8,128)S(1)}, f32[4,96,1024]{2,1,0:T(8,128)S(1)}) custom-call(s32[1]{0:T(128)} %bitcast.refs_0_, bf16[128,8192]{1,0:T(8,128)(2,1)S(1)} %copy-done, bf16[4,96,1024]{2,1,0:T(8,128)(2,1)S(1)} %all_to_all.43.refs_2_, bf16[4,96,1024]{2,1,0:T(8,128)(2,1)S(1)} %collective-permute-done.refs_3_), custom_call_target="tpu_custom_call" | custom-call | tf_op jit(solution)/shard_map/layer/pallas_call | solution.py:88
  69.1 2.3 %collective-permute-start.1 = (f32[4,96,1024]{2,1,0:T(8,128)S(1)}, f32[4,96,1024]{2,1,0:T(8,128)S(1)}, u32[]{:S(2)}, u32[]{:S(2)}) collective-permute-start(f32[4,96,1024]{2,1,0:T(8,128)S(1)} %get-tuple-element.6), channel_id=1, source_target_pairs={{0,1},{1,0},{2,3},{3,2},{4,5},{5,4},{6,7},{7,6},{8,9},{9,8},{10,11... | collective-permute-start | bytes 4718600 | tf_op jit(solution)/shard_map/ppermute | solution.py:98
  71.4 3.0 %collective-permute-done.1 = f32[4,96,1024]{2,1,0:T(8,128)S(1)} collective-permute-done((f32[4,96,1024]{2,1,0:T(8,128)S(1)}, f32[4,96,1024]{2,1,0:T(8,128)S(1)}, u32[]{:S(2)}, u32[]{:S(2)}) %collective-permute-start.1) | collective-permute-done | bytes 1572896 | tf_op jit(solution)/shard_map/ppermute | solution.py:98
  74.4 0.3 add_convert_fusion
  74.8 14.4 %all_to_all.44 = bf16[4,96,1024]{2,1,0:T(8,128)(2,1)S(1)} all-to-all(bf16[4,96,1024]{2,1,0:T(8,128)(2,1)S(1)} %add_convert_fusion), channel_id=1, replica_groups=mesh['y'=8,'zh'=4,'x'=4,'zl'=3,'c'=2] {'x'}, dimensions={0} | all-to-all | bytes 1572864 | tf_op jit(solution)/shard_map/all_to_all | solution.py:99
  89.2 0.1 reduce_sum.30
  89.4 0.1 reshape.48
  89.4 0.1 copy.14
  89.5 0.1 copy.15
  89.6 12.5 %all_to_all.45 = bf16[8,12,1024]{2,1,0:T(8,128)(2,1)S(1)} all-to-all(bf16[8,12,1024]{2,1,0:T(8,128)(2,1)S(1)} %copy.15), channel_id=1, replica_groups=mesh['y'=8,'zh'=4,'x'=4,'zl'=3,'c'=2] {'y'}, dimensions={0} | all-to-all | bytes 393216 | tf_op jit(solution)/shard_map/all_to_all | solution.py:102
  102.3 12.0 %all_to_all.46 = f32[12,1,1024]{2,1,0:T(1,128)S(1)} all-to-all(f32[12,1,1024]{2,1,0:T(1,128)S(1)} %all_to_all.31), channel_id=1, replica_groups=mesh['y'=8,'zh'=4,'x'=4,'zl'=3,'c'=2] {'zh','zl'}, dimensions={0} | all-to-all | bytes 98304 | tf_op jit(solution)/shard_map/all_to_all | solution.py:104
  114.3 0.1 broadcast_in_dim.31
  114.3 14.0 %all_to_all.47 = f32[24,1,1024]{2,1,0:T(1,128)S(1)} all-to-all(f32[24,1,1024]{2,1,0:T(1,128)S(1)} %broadcast_in_dim.31), channel_id=1, replica_groups=mesh['y'=8,'zh'=4,'x'=4,'zl'=3,'c'=2] {'x','zl','c'}, dimensions={0} | all-to-all | bytes 196608 | tf_op jit(solution)/shard_map/all_to_all | solution.py:17
  128.3 0.2 reduce.3
  128.6 0.1 reshape.50
  128.7 0.7 squeeze.11
  129.3 0.7 squeeze.10
  130.0 0.7 squeeze.9
  (12 shorter events, 0.3 us)
Async XLA Ops:
  44.0 21.1 %copy-start = (bf16[128,8192]{1,0:T(8,128)(2,1)S(1)}, bf16[128,8192]{1,0:T(8,128)(2,1)}, u32[]{:S(2)}) copy-start(bf16[128,8192]{1,0:T(8,128)(2,1)} %refs_1_.1) | copy-start | bytes 6291460
  56.4 8.7 %collective-permute-start = (bf16[4,96,1024]{2,1,0:T(8,128)(2,1)S(1)}, bf16[4,96,1024]{2,1,0:T(8,128)(2,1)S(1)}, u32[]{:S(2)}, u32[]{:S(2)}) collective-permute-start(bf16[4,96,1024]{2,1,0:T(8,128)(2,1)S(1)} %all_to_all.43.refs_2_), channel_id=1, source_target_pairs={{0,1},{1,0},{2,3},{3,2},{4,5},{5,4},{6,7},{7,6},{8,9},{9,8},{10,11... | collective-permute-start | bytes 2359304 | tf_op jit(solution)/shard_map/ppermute | solution.py:84
  69.1 5.3 %collective-permute-start.1 = (f32[4,96,1024]{2,1,0:T(8,128)S(1)}, f32[4,96,1024]{2,1,0:T(8,128)S(1)}, u32[]{:S(2)}, u32[]{:S(2)}) collective-permute-start(f32[4,96,1024]{2,1,0:T(8,128)S(1)} %get-tuple-element.6), channel_id=1, source_target_pairs={{0,1},{1,0},{2,3},{3,2},{4,5},{5,4},{6,7},{7,6},{8,9},{9,8},{10,11... | collective-permute-start | bytes 4718600 | tf_op jit(solution)/shard_map/ppermute | solution.py:98

commit v2 on v1

--- a/solution.py
+++ b/solution.py
@@ -7,8 +7,10 @@
 from jax.sharding import PartitionSpec as P
 
 BLK = ("y", "zh")
-Z = ("zh", "zl")
 REP = ("x", "zl", "c")
+PLANE = ("zl", "y", "zh")
+OWNERS = ("zl", "c", "x")
+TILE = (8, 128)
 NT = (((1,), (1,)), ((), ()))
 
 
@@ -76,10 +78,8 @@
 
     at = (core * xs + lax.axis_index("x")) * width
     mine = lax.select_n(lax.axis_index("zl"), gate_weight, up_weight, down_weight)
-    piece = lax.dynamic_slice(mine, (0, at), (1, width))
-    over_z = sent_to_all(piece[0], Z)
-    over_y = sent_to_all(over_z, "y").reshape(ys, zhs, zls, width)
-    plane = over_y.transpose(2, 0, 1, 3).reshape(rows, width)
+    piece = lax.dynamic_slice(mine, (0, at), (1, width)).reshape(TILE)
+    plane = sent_to_all(piece, PLANE).reshape(rows, width)
     own = sent_to_all(plane, "x")
     other = lax.ppermute(own, "c", swap)
 
@@ -98,13 +98,9 @@
     both = (keep + lax.ppermute(send, "c", swap)).astype(jnp.bfloat16)
     got = lax.all_to_all(both, "x", 0, 0, tiled=True)
     sum_x = got.astype(jnp.float32).sum(axis=0).astype(jnp.bfloat16)
-    by_y = sum_x.reshape(zls, ys, zhs, width).transpose(1, 2, 0, 3).reshape(ys, zhs * zls, width)
-    got = lax.all_to_all(by_y, "y", 0, 0, tiled=True)
-    sum_y = got.astype(jnp.float32).sum(axis=0)
-    got = lax.all_to_all(sum_y, Z, 0, 0, tiled=True)
-    total = got.sum(axis=0)
-    every = sent_to_all(total, REP).reshape(xs, zls, cs, width)
-    result = every.transpose(1, 2, 0, 3).reshape(zls, 1, features)
+    got = lax.all_to_all(sum_x.reshape(rows, *TILE), PLANE, 0, 0, tiled=True)
+    total = got.astype(jnp.float32).sum(axis=0)
+    result = sent_to_all(total, OWNERS).reshape(zls, 1, features)
     return (result[0], result[1], result[2])
 
 

time: 131 us -> 120 us (0.916)
  blocking collectives: 106 us -> 98.4 us
  local copies, waits for them, and re-layouts: 3.48 us -> 0.83 us
    all_to_all x4 -> x3, blocking collectives: 67.1 us -> 62.6 us  [sent_to_all(): lax.all_to_all(jnp.broadcast_to(x[None], (peers, *x.shape)), axis, 0, 0,...]
    all_to_all x2 -> x1, blocking collectives: 24.5 us -> 21.4 us  [per_device(): got = lax.all_to_all(sum_x.reshape(rows, *TILE), PLANE, 0, 0, tiled=True)]
    squeeze x3 -> x0, local copies, waits for them, and re-layouts: 1.99 us -> none  [per_device(): return (result[0], result[1], result[2])]
where the time goes in v2:
time: 120 us
  blocking collectives  98.4 us (82%)
  starting transfers between devices  9.51 us (8%)
  waiting for transfers between devices  4.91 us (4%)
  Pallas kernels  4.03 us (3%)
  other arithmetic  1.33 us (1%)
    all_to_all x3, blocking collectives, sent_to_all(): lax.all_to_all(jnp.broadcast_to(x[None], (peers, *x.shape)), axis, 0, 0,...  62.6 us
    all_to_all x1, blocking collectives, per_device(): got = lax.all_to_all(sum_x.reshape(rows, *TILE), PLANE, 0, 0, tiled=True)  21.4 us
    all_to_all x1, blocking collectives, per_device(): got = lax.all_to_all(both, 'x', 0, 0, tiled=True)  14.5 us
    ppermute x1, starting transfers between devices, per_device(): other = lax.ppermute(own, 'c', swap)  7.24 us
    pallas_call x1, Pallas kernels, per_device(): pl.pallas_call(lambda *refs: layer_kernel(loss_scale, *refs), out_shape=(...  4.03 us
    ppermute x1, waiting for transfers between devices, per_device(): both = (keep + lax.ppermute(send, 'c', swap)).astype(jnp.bfloat16)  3.02 us
  transfers between devices with their start and end apart: 2, of which 2 were waited for; matrix products, arithmetic and copies ran while one was open for 0% of the time, Pallas kernels for 0%

profile of v2, /device:TPU:1, one launch (start us, length us, event | category | flops | bytes accessed | tf_op | source)
XLA Modules:
  0.0 119.7 jit_solution(14753239334922424374)
XLA Ops:
  0.6 0.8 fusion
  1.4 36.5 %all_to_all.25 = bf16[96,8,128]{2,1,0:T(8,128)(2,1)S(1)} all-to-all(bf16[96,8,128]{2,1,0:T(8,128)(2,1)S(1)} %broadcast_in_dim.21), channel_id=1, replica_groups=mesh['y'=8,'zh'=4,'x'=4,'zl'=3,'c'=2] {'zl','y','zh'}, dimensions={0} | all-to-all | bytes 393216 | tf_op jit(solution)/shard_map/all_to_all | solution.py:19
  38.0 0.0 copy-start
  38.0 0.1 broadcast_in_dim.23
  38.1 12.3 %all_to_all.26.refs_2_ = bf16[4,96,1024]{2,1,0:T(8,128)(2,1)S(1)} all-to-all(bf16[4,96,1024]{2,1,0:T(8,128)(2,1)S(1)} %broadcast_in_dim.23), channel_id=1, replica_groups=mesh['y'=8,'zh'=4,'x'=4,'zl'=3,'c'=2] {'x'}, dimensions={0} | all-to-all | bytes 1572864 | tf_op jit(solution)/shard_map/all_to_all | solution.py:19
  50.4 7.2 %collective-permute-start = (bf16[4,96,1024]{2,1,0:T(8,128)(2,1)S(1)}, bf16[4,96,1024]{2,1,0:T(8,128)(2,1)S(1)}, u32[]{:S(2)}, u32[]{:S(2)}) collective-permute-start(bf16[4,96,1024]{2,1,0:T(8,128)(2,1)S(1)} %all_to_all.26.refs_2_), channel_id=1, source_target_pairs={{0,1},{1,0},{2,3},{3,2},{4,5},{5,4},{6,7},{7,6},{8,9},{9,8},{10,11... | collective-permute-start | bytes 2359304 | tf_op jit(solution)/shard_map/ppermute | solution.py:84
  57.6 1.9 %collective-permute-done.refs_3_ = bf16[4,96,1024]{2,1,0:T(8,128)(2,1)S(1)} collective-permute-done((bf16[4,96,1024]{2,1,0:T(8,128)(2,1)S(1)}, bf16[4,96,1024]{2,1,0:T(8,128)(2,1)S(1)}, u32[]{:S(2)}, u32[]{:S(2)}) %collective-permute-start) | collective-permute-done | bytes 786464 | tf_op jit(solution)/shard_map/ppermute | solution.py:84
  59.5 0.0 copy-done
  59.5 4.0 %layer.1 = (f32[4,96,1024]{2,1,0:T(8,128)S(1)}, f32[4,96,1024]{2,1,0:T(8,128)S(1)}) custom-call(s32[1]{0:T(128)} %bitcast.refs_0_, bf16[128,8192]{1,0:T(8,128)(2,1)S(1)} %copy-done, bf16[4,96,1024]{2,1,0:T(8,128)(2,1)S(1)} %all_to_all.26.refs_2_, bf16[4,96,1024]{2,1,0:T(8,128)(2,1)S(1)} %collective-permute-done.refs_3_), custom_call_target="tpu_custom_call" | custom-call | tf_op jit(solution)/shard_map/layer/pallas_call | solution.py:88
  63.5 2.3 %collective-permute-start.1 = (f32[4,96,1024]{2,1,0:T(8,128)S(1)}, f32[4,96,1024]{2,1,0:T(8,128)S(1)}, u32[]{:S(2)}, u32[]{:S(2)}) collective-permute-start(f32[4,96,1024]{2,1,0:T(8,128)S(1)} %get-tuple-element.6), channel_id=1, source_target_pairs={{0,1},{1,0},{2,3},{3,2},{4,5},{5,4},{6,7},{7,6},{8,9},{9,8},{10,11... | collective-permute-start | bytes 4718600 | tf_op jit(solution)/shard_map/ppermute | solution.py:98
  65.8 3.0 %collective-permute-done.1 = f32[4,96,1024]{2,1,0:T(8,128)S(1)} collective-permute-done((f32[4,96,1024]{2,1,0:T(8,128)S(1)}, f32[4,96,1024]{2,1,0:T(8,128)S(1)}, u32[]{:S(2)}, u32[]{:S(2)}) %collective-permute-start.1) | collective-permute-done | bytes 1572896 | tf_op jit(solution)/shard_map/ppermute | solution.py:98
  68.8 0.3 add_convert_fusion
  69.2 14.5 %all_to_all.27 = bf16[4,96,1024]{2,1,0:T(8,128)(2,1)S(1)} all-to-all(bf16[4,96,1024]{2,1,0:T(8,128)(2,1)S(1)} %add_convert_fusion), channel_id=1, replica_groups=mesh['y'=8,'zh'=4,'x'=4,'zl'=3,'c'=2] {'x'}, dimensions={0} | all-to-all | bytes 1572864 | tf_op jit(solution)/shard_map/all_to_all | solution.py:99
  83.6 0.1 reduce_sum.21
  83.8 21.4 %all_to_all.28 = bf16[96,8,128]{2,1,0:T(8,128)(2,1)S(1)} all-to-all(bf16[96,8,128]{2,1,0:T(8,128)(2,1)S(1)} %bitcast.13), channel_id=1, replica_groups=mesh['y'=8,'zh'=4,'x'=4,'zl'=3,'c'=2] {'zl','y','zh'}, dimensions={0} | all-to-all | bytes 393216 | tf_op jit(solution)/shard_map/all_to_all | solution.py:101
  105.2 0.1 convert_reduce_fusion
  105.3 13.8 %all_to_all.29 = f32[24,8,128]{2,1,0:T(8,128)S(1)} all-to-all(f32[24,8,128]{2,1,0:T(8,128)S(1)} %broadcast_in_dim.24), channel_id=1, replica_groups=mesh['y'=8,'zh'=4,'x'=4,'zl'=3,'c'=2] {'zl','c','x'}, dimensions={0} | all-to-all | bytes 196608 | tf_op jit(solution)/shard_map/all_to_all | solution.py:19
  119.1 0.6 fusion.1
  (4 shorter events, 0.1 us)
Async XLA Ops:
  38.0 21.6 %copy-start = (bf16[128,8192]{1,0:T(8,128)(2,1)S(1)}, bf16[128,8192]{1,0:T(8,128)(2,1)}, u32[]{:S(2)}) copy-start(bf16[128,8192]{1,0:T(8,128)(2,1)} %refs_1_.1) | copy-start | bytes 6291460
  50.4 9.1 %collective-permute-start = (bf16[4,96,1024]{2,1,0:T(8,128)(2,1)S(1)}, bf16[4,96,1024]{2,1,0:T(8,128)(2,1)S(1)}, u32[]{:S(2)}, u32[]{:S(2)}) collective-permute-start(bf16[4,96,1024]{2,1,0:T(8,128)(2,1)S(1)} %all_to_all.26.refs_2_), channel_id=1, source_target_pairs={{0,1},{1,0},{2,3},{3,2},{4,5},{5,4},{6,7},{7,6},{8,9},{9,8},{10,11... | collective-permute-start | bytes 2359304 | tf_op jit(solution)/shard_map/ppermute | solution.py:84
  63.5 5.3 %collective-permute-start.1 = (f32[4,96,1024]{2,1,0:T(8,128)S(1)}, f32[4,96,1024]{2,1,0:T(8,128)S(1)}, u32[]{:S(2)}, u32[]{:S(2)}) collective-permute-start(f32[4,96,1024]{2,1,0:T(8,128)S(1)} %get-tuple-element.6), channel_id=1, source_target_pairs={{0,1},{1,0},{2,3},{3,2},{4,5},{5,4},{6,7},{7,6},{8,9},{9,8},{10,11... | collective-permute-start | bytes 4718600 | tf_op jit(solution)/shard_map/ppermute | solution.py:98

commit v3 on v2

v3 whole, which is shorter than its diff:
```python
import jax
import jax.numpy as jnp
from jax import lax
from jax.experimental import pallas as pl
from jax.experimental.pallas import tpu as pltpu
from jax.sharding import Mesh
from jax.sharding import PartitionSpec as P

BLK = ("y", "zh")
REP = ("x", "zl", "c")
PLANE = ("zl", "y", "zh")
OWNERS = ("zl", "c", "x")
ROW_TILE = (8, 128)
HIGH, LANES = 16, 128
NT = (((1,), (1,)), ((), ()))
F32, BF16 = jnp.float32, jnp.bfloat16


def sent_to_all(x, axis):
    peers = lax.axis_size(axis)
    return lax.all_to_all(jnp.broadcast_to(x[None], (peers, *x.shape)), axis, 0, 0, tiled=True)


def halves(square):
    high = square.astype(BF16).astype(F32)
    return high, (square - high).astype(BF16).astype(F32)


def square_to_tile(square):
    n = square.shape[0]
    high, low = halves(square)
    parts = []
    for at in range(0, n, HIGH):
        parts += [high[at : at + HIGH], low[at : at + HIGH]]
    if (spare := LANES - 2 * n * (n // HIGH)) > 0:
        parts.append(jnp.zeros((HIGH, spare), F32))
    return jnp.concatenate(parts, axis=1).astype(BF16)


def tile_to_square(tile, n):
    wide = tile.astype(F32)
    rows = []
    for group in range(n // HIGH):
        at = 2 * n * group
        rows.append(wide[:, at : at + n] + wide[:, at + n : at + 2 * n])
    return jnp.concatenate(rows, axis=0)


def places(rows, width):
    return [
        (slice(r, r + HIGH), slice(c, c + LANES))
        for r in range(0, rows, HIGH)
        for c in range(0, width, LANES)
    ]


def from_tiles(ref, part, rows, width):
    across = width // LANES
    return jnp.concatenate(
        [
            jnp.concatenate([ref[part, r * across + c] for c in range(across)], axis=1)
            for r in range(rows // HIGH)
        ],
        axis=0,
    )


def pack_kernel(plane_ref, out_ref):
    rows, width = plane_ref.shape
    two = 2 * rows // 3
    peers = out_ref.shape[0]
    down = plane_ref[two:, :]
    square = square_to_tile(lax.dot_general(down, down, NT, preferred_element_type=F32))
    for at, (r, c) in enumerate(places(two, width)):
        tile = plane_ref[r, c]
        for p in range(peers):
            out_ref[p, at] = tile
    for p in range(peers):
        out_ref[p, out_ref.shape[1] - 1] = square


def token_columns(core, part, tok_ref, got_ref, parts):
    width = got_ref.shape[1] // parts
    own = tok_ref[:, pl.ds(pl.multiple_of(core * got_ref.shape[1] + part * width, width), width)]
    return jnp.concatenate([own, got_ref[:, part * width : (part + 1) * width]], axis=0)


def pre_kernel(core_ref, tok_ref, got_ref, w_ref, out_ref):
    parts, tiles = w_ref.shape[:2]
    width = got_ref.shape[1] // parts
    two = (tiles - 1) * HIGH * LANES // width
    hid = two // 2
    core = core_ref[0]
    pre = jnp.zeros((2 * tok_ref.shape[0], two), F32)
    square = jnp.zeros((hid, hid), F32)
    for part in range(parts):
        pre += lax.dot_general(
            token_columns(core, part, tok_ref, got_ref, parts),
            from_tiles(w_ref, part, two, width),
            NT,
            preferred_element_type=F32,
        )
        square += tile_to_square(w_ref[part, tiles - 1], hid)
    out_ref[:two, :] = pre.T
    blank = jnp.zeros((hid, out_ref.shape[1] - hid), F32)
    out_ref[two:, :] = jnp.concatenate([square, blank], axis=1)


def grad_kernel(loss_scale, core_ref, tok_ref, got_ref, own_ref, other_ref, out_ref):
    parts, tiles = out_ref.shape[:2]
    width = got_ref.shape[1] // parts
    two = (tiles - 1) * HIGH * LANES // width
    hid = two // 2
    toks = tok_ref.shape[0]
    core = core_ref[0]
    other = jnp.concatenate([other_ref[:two, toks:], other_ref[:two, :toks]], axis=1)
    pre = own_ref[:two, :] + other
    high, low = halves(own_ref[two:, :hid] + other_ref[two:, :hid])
    gate_pre = pre[:hid]
    up_pre = pre[hid:]
    sigmoid_gate = jax.nn.sigmoid(gate_pre)
    active = gate_pre * sigmoid_gate
    hidden = (active * up_pre).astype(BF16)
    hidden_grad = loss_scale * (
        jnp.dot(high.astype(BF16), hidden, preferred_element_type=F32)
        + jnp.dot(low.astype(BF16), hidden, preferred_element_type=F32)
    )
    gate_grad = hidden_grad * up_pre * (sigmoid_gate * (1.0 + gate_pre * (1.0 - sigmoid_gate)))
    up_grad = hidden_grad * active
    grads = jnp.concatenate([gate_grad, up_grad], axis=0).astype(BF16)
    square = square_to_tile(lax.dot_general(hidden, hidden, NT, preferred_element_type=F32))
    for part in range(parts):
        terms = jnp.dot(
            grads,
            token_columns(core, part, tok_ref, got_ref, parts),
            preferred_element_type=F32,
        ).astype(BF16)
        for at, (r, c) in enumerate(places(two, width)):
            out_ref[part, at] = terms[r, c]
        out_ref[part, tiles - 1] = square


def sum_kernel(got_ref, out_ref):
    parts, tiles = got_ref.shape[:2]
    rows, width = out_ref.shape
    two = 2 * rows // 3
    hid = two // 2
    for at, (r, c) in enumerate(places(two, width)):
        total = got_ref[0, at].astype(F32)
        for p in range(1, parts):
            total += got_ref[p, at].astype(F32)
        out_ref[r, c] = total.astype(BF16)
    square = tile_to_square(got_ref[0, tiles - 1], hid)
    for p in range(1, parts):
        square += tile_to_square(got_ref[p, tiles - 1], hid)
    blank = jnp.zeros((hid, LANES - hid), F32)
    high, low = halves(square)
    both = [jnp.concatenate([half, blank], axis=1).astype(BF16) for half in (high, low)]
    out_ref[two:, : 2 * LANES] = jnp.concatenate(both, axis=1)
    out_ref[two:, 2 * LANES :] = jnp.zeros((hid, width - 2 * LANES), BF16)


def final_kernel(loss_scale, kind_ref, got_ref, gathered_ref, out_ref):
    total = got_ref[0].astype(F32)
    for at in range(1, got_ref.shape[0]):
        total += got_ref[at].astype(F32)
    hid = gathered_ref.shape[0] // 3

    @pl.when(kind_ref[0] != 2)
    def _():
        for to in range(out_ref.shape[0]):
            out_ref[to] = total

    @pl.when(kind_ref[0] == 2)
    def _():
        row = (total[0:1] + total[1:2]) * loss_scale
        result = jnp.zeros(total.shape, F32)
        for at in range(hid):
            factor = jnp.broadcast_to(row[:, at : at + 1], total.shape)
            result += factor * gathered_ref[2 * hid + at].astype(F32)
        for to in range(out_ref.shape[0]):
            out_ref[to] = result


def call(kernel, name, shape, dtype, *args):
    vmem = pl.BlockSpec(memory_space=pltpu.VMEM)
    smem = pl.BlockSpec(memory_space=pltpu.SMEM)
    return pl.pallas_call(
        kernel,
        out_shape=jax.ShapeDtypeStruct(shape, dtype),
        in_specs=[smem if a.dtype == jnp.int32 else vmem for a in args],
        out_specs=vmem,
        compiler_params=pltpu.CompilerParams(vmem_limit_bytes=32 << 20),
        name=name,
    )(*args)


def per_device(tokens, gate_weight, up_weight, down_weight):
    ys, zhs, xs, zls, cs = (lax.axis_size(a) for a in ("y", "zh", "x", "zl", "c"))
    tok_rows, features = tokens.shape
    devices = ys * zhs * xs * zls * cs
    loss_scale = float(tok_rows * devices) ** (-0.5)
    width = features // (xs * cs)
    rows = 3 * ys * zhs
    two = 2 * rows // 3
    tiles = two * width // (HIGH * LANES) + 1
    core = lax.axis_index("c")
    kind = lax.axis_index("zl")
    swap = [(i, (i + 1) % cs) for i in range(cs)]
    side = features // cs

    sent = lax.dynamic_slice(tokens, (0, (1 - core) * side), (tok_rows, side))
    got_tokens = lax.ppermute(sent, "c", swap)

    at = (core * xs + lax.axis_index("x")) * width
    mine = lax.select_n(kind, gate_weight, up_weight, down_weight)
    piece = lax.dynamic_slice(mine, (0, at), (1, width)).reshape(ROW_TILE)
    gathered = sent_to_all(piece, PLANE)
    packed = call(
        pack_kernel, "pack", (xs, tiles, HIGH, LANES), BF16, gathered.reshape(rows, width)
    )
    weights = lax.all_to_all(packed, "x", 0, 0, tiled=True)

    which = core.reshape(1)
    pre = call(
        pre_kernel, "pre", (rows, cs * tok_rows), F32, which, tokens, got_tokens, weights
    )
    other = lax.ppermute(pre, "c", swap)
    terms = call(
        lambda *refs: grad_kernel(loss_scale, *refs),
        "grad",
        (xs, tiles, HIGH, LANES),
        BF16,
        which,
        tokens,
        got_tokens,
        pre,
        other,
    )
    got = lax.all_to_all(terms, "x", 0, 0, tiled=True)
    sums = call(sum_kernel, "sums", (rows, width), BF16, got)
    got = lax.all_to_all(sums.reshape(rows, *ROW_TILE), PLANE, 0, 0, tiled=True)
    every = call(
        lambda *refs: final_kernel(loss_scale, *refs),
        "final",
        (xs * zls * cs, *ROW_TILE),
        F32,
        kind.reshape(1),
        got,
        gathered,
    )
    result = lax.all_to_all(every, OWNERS, 0, 0, tiled=True).reshape(zls, 1, features)
    return (result[0], result[1], result[2])


def split_mesh(mesh, shape):
    return Mesh(mesh.devices.reshape(shape), ("y", "zh", "x", "zl", "c"))


def solution(mesh):
    return jax.shard_map(
        per_device,
        mesh=split_mesh(mesh, (8, 4, 4, 3, 2)),
        in_specs=(P(BLK + REP, None), P(BLK, None), P(BLK, None), P(BLK, None)),
        out_specs=(P(BLK, None), P(BLK, None), P(BLK, None)),
        check_vma=False,
    )
```

time: 120 us -> 112 us (0.933)
  blocking collectives: 98.4 us -> 86.1 us
  starting transfers between devices: 9.51 us -> 17.7 us
  waiting for transfers between devices: 4.91 us -> 0.92 us
  local copies, waits for them, and re-layouts: 0.83 us -> 3.18 us
  Pallas kernels: 4.03 us -> 1.84 us
    all_to_all x3 -> x1, blocking collectives: 62.6 us -> 27.8 us  [sent_to_all(): lax.all_to_all(jnp.broadcast_to(x[None], (peers, *x.shape)), axis, 0, 0,...]
    all_to_all x2 -> x4, blocking collectives: 35.8 us -> 58.2 us  [the longest x1 21.5 us: per_device(): got = lax.all_to_all(sums.reshape(rows, *ROW_TILE), PLANE, 0, 0, tiled=True)]
    ppermute x2, starting transfers between devices: 9.51 us -> 17.7 us  [the longest x1 12.4 us: per_device(): got_tokens = lax.ppermute(sent, 'c', swap)]
    ppermute x2, waiting for transfers between devices: 4.91 us -> 0.92 us  [the longest x1 0.92 us: per_device(): other = lax.ppermute(pre, 'c', swap)]
    dynamic_slice x0 -> x1, local copies, waits for them, and re-layouts: none -> 2.45 us  [per_device(): sent = lax.dynamic_slice(tokens, (0, (1 - core) * side), (tok_rows, side))]
    pallas_call x1 -> x5, Pallas kernels: 4.03 us -> 1.84 us  [call(): pl.pallas_call(kernel, out_shape=jax.ShapeDtypeStruct(shape, dtype), in_s...]
  transfers between devices with their start and end apart: 2 -> 2, of which waited for: 2 -> 1; matrix products, arithmetic and copies ran while one was open for 0% -> 1% of each run, Pallas kernels for 0% -> 0%
where the time goes in v3:
time: 112 us; the launch traced here: 111 us
  blocking collectives  86.1 us (77%)
  starting transfers between devices  17.7 us (16%)
  local copies, waits for them, and re-layouts  3.18 us (3%)
  Pallas kernels  1.84 us (2%)
    all_to_all x1, blocking collectives, sent_to_all(): lax.all_to_all(jnp.broadcast_to(x[None], (peers, *x.shape)), axis, 0, 0,...  27.8 us
    all_to_all x1, blocking collectives, per_device(): got = lax.all_to_all(sums.reshape(rows, *ROW_TILE), PLANE, 0, 0, tiled=True)  21.5 us
    all_to_all x1, blocking collectives, per_device(): lax.all_to_all(every, OWNERS, 0, 0, tiled=True).reshape(zls, 1, features)  13.9 us
    ppermute x1, starting transfers between devices, per_device(): got_tokens = lax.ppermute(sent, 'c', swap)  12.4 us
    all_to_all x1, blocking collectives, per_device(): got = lax.all_to_all(terms, 'x', 0, 0, tiled=True)  11.8 us
    all_to_all x1, blocking collectives, per_device(): weights = lax.all_to_all(packed, 'x', 0, 0, tiled=True)  11.1 us
    ppermute x1, starting transfers between devices, per_device(): other = lax.ppermute(pre, 'c', swap)  5.26 us
    dynamic_slice x1, local copies, waits for them, and re-layouts, per_device(): sent = lax.dynamic_slice(tokens, (0, (1 - core) * side), (tok_rows, side))  2.45 us
  transfers between devices with their start and end apart: 2, of which 1 were waited for; matrix products, arithmetic and copies ran while one was open for 1% of the time, Pallas kernels for 0%

profile of v3, /device:TPU:1, one launch (start us, length us, event | category | flops | bytes accessed | tf_op | source)
XLA Modules:
  0.0 111.1 jit_solution(16060808678920611274)
XLA Ops:
  0.6 0.0 copy-start
  0.6 2.4 %constant_dynamic-slice_fusion = bf16[128,4096]{1,0:T(8,128)(2,1)} fusion(bf16[128,8192]{1,0:T(8,128)(2,1)} %refs_1_.1, s32[]{:T(128)S(6)} %select_n.24), kind=kLoop, calls=%fused_computation.4 | loop fusion | bytes 2097156 | tf_op jit(solution)/shard_map/dynamic_slice | solution.py:212
  3.1 12.4 %collective-permute-start = (bf16[128,4096]{1,0:T(8,128)(2,1)}, bf16[128,4096]{1,0:T(8,128)(2,1)S(1)}, u32[]{:S(2)}, u32[]{:S(2)}) collective-permute-start(bf16[128,4096]{1,0:T(8,128)(2,1)} %constant_dynamic-slice_fusion), channel_id=1, source_target_pairs={{0,1},{1,0},{2,3},{3,2},{4,5},{5,4},{6,7},{7,6},{8,9},{9,8},{10,11... | collective-permute-start | bytes 3145736 | tf_op jit(solution)/shard_map/ppermute | solution.py:213
  15.5 0.8 fusion
  16.3 27.8 %all_to_all.25.refs_2_ = bf16[96,8,128]{2,1,0:T(8,128)(2,1)S(1)} all-to-all(bf16[96,8,128]{2,1,0:T(8,128)(2,1)S(1)} %broadcast_in_dim.8), channel_id=1, replica_groups=mesh['y'=8,'zh'=4,'x'=4,'zl'=3,'c'=2] {'zl','y','zh'}, dimensions={0} | all-to-all | bytes 393216 | tf_op jit(solution)/shard_map/all_to_all | solution.py:21
  44.2 0.3 pack.1
  44.4 11.1 %all_to_all.26.w_ref = bf16[4,33,16,128]{3,2,1,0:T(8,128)(2,1)S(1)} all-to-all(bf16[4,33,16,128]{3,2,1,0:T(8,128)(2,1)S(1)} %pack.1), channel_id=1, replica_groups=mesh['y'=8,'zh'=4,'x'=4,'zl'=3,'c'=2] {'x'}, dimensions={0} | all-to-all | bytes 1081344 | tf_op jit(solution)/shard_map/all_to_all | solution.py:222
  55.5 0.0 collective-permute-done.got_ref.refs_2_
  55.5 0.0 copy-done
  55.5 0.7 pre.1.refs_3_
  56.2 5.3 %collective-permute-start.1 = (f32[96,256]{1,0:T(8,128)S(1)}, f32[96,256]{1,0:T(8,128)S(1)}, u32[]{:S(2)}, u32[]{:S(2)}) collective-permute-start(f32[96,256]{1,0:T(8,128)S(1)} %pre.1.refs_3_), channel_id=1, source_target_pairs={{0,1},{1,0},{2,3},{3,2},{4,5},{5,4},{6,7},{7,6},{8,9},{9,8},{10,11... | collective-permute-start | bytes 294920 | tf_op jit(solution)/shard_map/ppermute | solution.py:228
  61.5 0.9 collective-permute-done.1.refs_4_
  62.4 0.6 grad.1
  63.0 11.8 %all_to_all.27.got_ref = bf16[4,33,16,128]{3,2,1,0:T(8,128)(2,1)S(1)} all-to-all(bf16[4,33,16,128]{3,2,1,0:T(8,128)(2,1)S(1)} %grad.1), channel_id=1, replica_groups=mesh['y'=8,'zh'=4,'x'=4,'zl'=3,'c'=2] {'x'}, dimensions={0} | all-to-all | bytes 1081344 | tf_op jit(solution)/shard_map/all_to_all | solution.py:240
  74.8 0.1 sums.1
  75.0 21.5 %all_to_all.28.refs_1_ = bf16[96,8,128]{2,1,0:T(8,128)(2,1)S(1)} all-to-all(bf16[96,8,128]{2,1,0:T(8,128)(2,1)S(1)} %bitcast.15), channel_id=1, replica_groups=mesh['y'=8,'zh'=4,'x'=4,'zl'=3,'c'=2] {'zl','y','zh'}, dimensions={0} | all-to-all | bytes 393216 | tf_op jit(solution)/shard_map/all_to_all | solution.py:242
  96.5 0.1 final.1
  96.6 13.9 %all_to_all.29 = f32[24,8,128]{2,1,0:T(8,128)S(1)} all-to-all(f32[24,8,128]{2,1,0:T(8,128)S(1)} %final.1), channel_id=1, replica_groups=mesh['y'=8,'zh'=4,'x'=4,'zl'=3,'c'=2] {'zl','c','x'}, dimensions={0} | all-to-all | bytes 196608 | tf_op jit(solution)/shard_map/all_to_all | solution.py:252
  110.5 0.6 fusion.1
  (3 shorter events, 0.1 us)
Async XLA Ops:
  0.6 54.8 %copy-start = (bf16[128,8192]{1,0:T(8,128)(2,1)S(1)}, bf16[128,8192]{1,0:T(8,128)(2,1)}, u32[]{:S(2)}) copy-start(bf16[128,8192]{1,0:T(8,128)(2,1)} %refs_1_.1) | copy-start | bytes 6291460
  3.1 52.4 %collective-permute-start = (bf16[128,4096]{1,0:T(8,128)(2,1)}, bf16[128,4096]{1,0:T(8,128)(2,1)S(1)}, u32[]{:S(2)}, u32[]{:S(2)}) collective-permute-start(bf16[128,4096]{1,0:T(8,128)(2,1)} %constant_dynamic-slice_fusion), channel_id=1, source_target_pairs={{0,1},{1,0},{2,3},{3,2},{4,5},{5,4},{6,7},{7,6},{8,9},{9,8},{10,11... | collective-permute-start | bytes 3145736 | tf_op jit(solution)/shard_map/ppermute | solution.py:213
  56.2 6.2 %collective-permute-start.1 = (f32[96,256]{1,0:T(8,128)S(1)}, f32[96,256]{1,0:T(8,128)S(1)}, u32[]{:S(2)}, u32[]{:S(2)}) collective-permute-start(f32[96,256]{1,0:T(8,128)S(1)} %pre.1.refs_3_), channel_id=1, source_target_pairs={{0,1},{1,0},{2,3},{3,2},{4,5},{5,4},{6,7},{7,6},{8,9},{9,8},{10,11... | collective-permute-start | bytes 294920 | tf_op jit(solution)/shard_map/ppermute | solution.py:228

commit v4 on v3

v4 whole, which is shorter than its diff:
```python
import jax
import jax.numpy as jnp
from jax import lax
from jax.experimental import pallas as pl
from jax.experimental.pallas import tpu as pltpu
from jax.sharding import Mesh
from jax.sharding import PartitionSpec as P

AXES = ("yh", "yl", "zh", "x", "zl", "c")
BLK = AXES[:3]
PLANE = ("zl", "yl", "yh", "zh")
NEAR = ("x", "yl")
FAR = ("zl", "yh", "zh")
OWNERS = ("zl", "c", "x")
ROW_TILE = (8, 128)
HIGH, LANES = 16, 128
NT = (((1,), (1,)), ((), ()))
F32, BF16 = jnp.float32, jnp.bfloat16
VMEM = pl.BlockSpec(memory_space=pltpu.VMEM)
SMEM = pl.BlockSpec(memory_space=pltpu.SMEM)


def sent_to_all(x, axis):
    peers = lax.axis_size(axis)
    return lax.all_to_all(jnp.broadcast_to(x[None], (peers, *x.shape)), axis, 0, 0, tiled=True)


def halves(square):
    high = square.astype(BF16).astype(F32)
    return high, (square - high).astype(BF16).astype(F32)


def square_to_tile(square):
    m, n = square.shape
    high, low = halves(square)
    parts = []
    for at in range(0, m, HIGH):
        parts += [high[at : at + HIGH], low[at : at + HIGH]]
    if (spare := LANES - 2 * n * (m // HIGH)) > 0:
        parts.append(jnp.zeros((HIGH, spare), F32))
    return jnp.concatenate(parts, axis=1).astype(BF16)


def tile_to_square(tile, m, n):
    wide = tile.astype(F32)
    rows = []
    for group in range(m // HIGH):
        at = 2 * n * group
        rows.append(wide[:, at : at + n] + wide[:, at + n : at + 2 * n])
    return jnp.concatenate(rows, axis=0)


def places(rows, width):
    return [
        (slice(r, r + HIGH), slice(c, c + LANES))
        for r in range(0, rows, HIGH)
        for c in range(0, width, LANES)
    ]


def from_tiles(ref, part, rows, width):
    across = width // LANES
    return jnp.concatenate(
        [
            jnp.concatenate([ref[part, r * across + c] for c in range(across)], axis=1)
            for r in range(rows // HIGH)
        ],
        axis=0,
    )


def pack_kernel(plane_ref, out_ref):
    rows, width = plane_ref.shape
    two = 2 * rows // 3
    peers = out_ref.shape[0]
    down = plane_ref[two:, :]
    square = square_to_tile(lax.dot_general(down, down, NT, preferred_element_type=F32))
    for at, (r, c) in enumerate(places(two, width)):
        tile = plane_ref[r, c]
        for p in range(peers):
            out_ref[p, at] = tile
    for p in range(peers):
        out_ref[p, out_ref.shape[1] - 1] = square


def own_columns(core, part, parts, width):
    return pl.ds(pl.multiple_of((core * parts + part) * width, width), width)


def pre_kernel(width, core_ref, tok_ref, got_ref, w_ref, out_ref, half_ref, sem):
    parts, tiles = w_ref.shape[:2]
    two = (tiles - 1) * HIGH * LANES // width
    hid = two // 2
    core = core_ref[0]
    side = half_ref.shape[1]
    copy = pltpu.make_async_copy(
        got_ref.at[:, pl.ds(pl.multiple_of(core * side, side), side)], half_ref, sem
    )
    copy.start()
    weights = [from_tiles(w_ref, part, two, width) for part in range(parts)]
    square = jnp.zeros((hid, hid), F32)
    own = jnp.zeros((tok_ref.shape[0], two), F32)
    for part in range(parts):
        own += lax.dot_general(
            tok_ref[:, own_columns(core, part, parts, width)],
            weights[part],
            NT,
            preferred_element_type=F32,
        )
        square += tile_to_square(w_ref[part, tiles - 1], hid, hid)
    copy.wait()
    other = jnp.zeros((tok_ref.shape[0], two), F32)
    for part in range(parts):
        other += lax.dot_general(
            half_ref[:, part * width : (part + 1) * width],
            weights[part],
            NT,
            preferred_element_type=F32,
        )
    out_ref[:two, :] = jnp.concatenate([own, other], axis=0).T
    blank = jnp.zeros((hid, out_ref.shape[1] - hid), F32)
    out_ref[two:, :] = jnp.concatenate([square, blank], axis=1)


def grad_kernel(loss_scale, width, parts, core_ref, tok_ref, half_ref, own_ref, other_ref, out_ref):
    peers, tiles = out_ref.shape[:2]
    lanes = peers // parts
    hid = own_ref.shape[0] // 3
    two = 2 * hid
    share = hid // lanes
    toks = tok_ref.shape[0]
    core = core_ref[0]
    other = jnp.concatenate([other_ref[:two, toks:], other_ref[:two, :toks]], axis=1)
    pre = own_ref[:two, :] + other
    high, low = halves(own_ref[two:, :hid] + other_ref[two:, :hid])
    gate_pre = pre[:hid]
    up_pre = pre[hid:]
    sigmoid_gate = jax.nn.sigmoid(gate_pre)
    active = gate_pre * sigmoid_gate
    hidden = (active * up_pre).astype(BF16)
    hidden_grad = loss_scale * (
        jnp.dot(high.astype(BF16), hidden, preferred_element_type=F32)
        + jnp.dot(low.astype(BF16), hidden, preferred_element_type=F32)
    )
    gate_grad = hidden_grad * up_pre * (sigmoid_gate * (1.0 + gate_pre * (1.0 - sigmoid_gate)))
    up_grad = hidden_grad * active
    grads = jnp.concatenate([gate_grad, up_grad], axis=0).astype(BF16)
    square = lax.dot_general(hidden, hidden, NT, preferred_element_type=F32)
    squares = [square_to_tile(square[k * share : (k + 1) * share]) for k in range(lanes)]
    for part in range(parts):
        own = tok_ref[:, own_columns(core, part, parts, width)]
        chip = jnp.concatenate([own, half_ref[:, part * width : (part + 1) * width]], axis=0)
        terms = jnp.dot(grads, chip, preferred_element_type=F32).astype(BF16)
        for lane in range(lanes):
            to = part * lanes + lane
            for at, (r, c) in enumerate(places(2 * share, width)):
                which, row = divmod(r.start, share)
                first = which * hid + lane * share + row
                out_ref[to, at] = terms[first : first + HIGH, c]
            out_ref[to, tiles - 1] = squares[lane]


def sum_kernel(hid, got_ref, out_ref):
    peers, tiles = got_ref.shape[:2]
    rows, width = out_ref.shape
    two = 2 * rows // 3
    share = two // 2
    for at, (r, c) in enumerate(places(two, width)):
        total = got_ref[0, at].astype(F32)
        for p in range(1, peers):
            total += got_ref[p, at].astype(F32)
        out_ref[r, c] = total.astype(BF16)
    square = tile_to_square(got_ref[0, tiles - 1], share, hid)
    for p in range(1, peers):
        square += tile_to_square(got_ref[p, tiles - 1], share, hid)
    blank = jnp.zeros((share, LANES - hid), F32)
    high, low = halves(square)
    both = [jnp.concatenate([half, blank], axis=1).astype(BF16) for half in (high, low)]
    out_ref[two:, : 2 * LANES] = jnp.concatenate(both, axis=1)
    out_ref[two:, 2 * LANES :] = jnp.zeros((share, width - 2 * LANES), BF16)


def final_kernel(loss_scale, kind_ref, got_ref, gathered_ref, out_ref):
    total = got_ref[0].astype(F32)
    for at in range(1, got_ref.shape[0]):
        total += got_ref[at].astype(F32)
    hid = gathered_ref.shape[0] // 3

    @pl.when(kind_ref[0] != 2)
    def _():
        for to in range(out_ref.shape[0]):
            out_ref[to] = total

    @pl.when(kind_ref[0] == 2)
    def _():
        row = (total[0:1] + total[1:2]) * loss_scale
        result = jnp.zeros(total.shape, F32)
        for at in range(hid):
            factor = jnp.broadcast_to(row[:, at : at + 1], total.shape)
            result += factor * gathered_ref[2 * hid + at].astype(F32)
        for to in range(out_ref.shape[0]):
            out_ref[to] = result


def call(kernel, name, shape, dtype, *args):
    return pl.pallas_call(
        kernel,
        out_shape=jax.ShapeDtypeStruct(shape, dtype),
        in_specs=[SMEM if a.dtype == jnp.int32 else VMEM for a in args],
        out_specs=VMEM,
        compiler_params=pltpu.CompilerParams(vmem_limit_bytes=32 << 20),
        name=name,
    )(*args)


def per_device(tokens, gate_weight, up_weight, down_weight):
    xs, cs, yls, zls = (lax.axis_size(a) for a in ("x", "c", "yl", "zl"))
    tok_rows, features = tokens.shape
    hid = lax.axis_size(BLK)
    loss_scale = float(tok_rows * lax.axis_size(AXES)) ** (-0.5)
    width = features // (xs * cs)
    rows = 3 * hid
    tiles = 2 * hid * width // (HIGH * LANES)
    core = lax.axis_index("c")
    kind = lax.axis_index("zl")
    swap = [(i, (i + 1) % cs) for i in range(cs)]

    got_tokens = lax.ppermute(tokens, "c", swap)

    at = (core * xs + lax.axis_index("x")) * width
    mine = lax.select_n(kind, gate_weight, up_weight, down_weight)
    piece = lax.dynamic_slice(mine, (0, at), (1, width)).reshape(ROW_TILE)
    gathered = sent_to_all(piece, PLANE)
    packed = call(
        pack_kernel,
        "pack",
        (xs, tiles + 1, HIGH, LANES),
        BF16,
        gathered.reshape(rows, width),
    )
    weights = lax.all_to_all(packed, "x", 0, 0, tiled=True)

    which = core.reshape(1)
    pre, half = pl.pallas_call(
        lambda *refs: pre_kernel(width, *refs),
        out_shape=(
            jax.ShapeDtypeStruct((rows, cs * tok_rows), F32),
            jax.ShapeDtypeStruct((tok_rows, features // cs), BF16),
        ),
        in_specs=[SMEM, VMEM, pl.BlockSpec(memory_space=pl.ANY), VMEM],
        out_specs=(VMEM, VMEM),
        scratch_shapes=[pltpu.SemaphoreType.DMA],
        compiler_params=pltpu.CompilerParams(vmem_limit_bytes=32 << 20),
        name="pre",
    )(which, tokens, got_tokens, weights)
    other = lax.ppermute(pre, "c", swap)
    terms = call(
        lambda *refs: grad_kernel(loss_scale, width, xs, *refs),
        "grad",
        (xs * yls, tiles // yls + 1, HIGH, LANES),
        BF16,
        which,
        tokens,
        half,
        pre,
        other,
    )
    got = lax.all_to_all(terms, NEAR, 0, 0, tiled=True)
    sums = call(lambda *refs: sum_kernel(hid, *refs), "sums", (rows // yls, width), BF16, got)
    got = lax.all_to_all(sums.reshape(-1, *ROW_TILE), FAR, 0, 0, tiled=True)
    every = call(
        lambda *refs: final_kernel(loss_scale, *refs),
        "final",
        (xs * zls * cs, *ROW_TILE),
        F32,
        kind.reshape(1),
        got,
        gathered,
    )
    result = lax.all_to_all(every, OWNERS, 0, 0, tiled=True).reshape(zls, 1, features)
    return (result[0], result[1], result[2])


def solution(mesh):
    split = Mesh(mesh.devices.reshape(4, 2, 4, 4, 3, 2), AXES)
    return jax.shard_map(
        per_device,
        mesh=split,
        in_specs=(P(AXES, None), P(BLK, None), P(BLK, None), P(BLK, None)),
        out_specs=(P(BLK, None), P(BLK, None), P(BLK, None)),
        check_vma=False,
    )
```

time: 112 us -> 110 us (0.982)
  local copies, waits for them, and re-layouts: 3.18 us -> 0.72 us
  blocking collectives: 86.1 us -> 84.2 us
  Pallas kernels: 1.84 us -> 3.48 us
    pallas_call x0 -> x1, Pallas kernels: none -> 2.48 us  [per_device(): pl.pallas_call(lambda *refs: pre_kernel(width, *refs), out_shape=(jax.Sha...]
    dynamic_slice x1 -> x0, local copies, waits for them, and re-layouts: 2.45 us -> none  [per_device(): sent = lax.dynamic_slice(tokens, (0, (1 - core) * side), (tok_rows, side))]
    all_to_all x2, blocking collectives: 33.3 us -> 31.8 us  [the longest x1 19.1 us: per_device(): got = lax.all_to_all(sums.reshape(-1, *ROW_TILE), FAR, 0, 0, tiled=True)]
where the time goes in v4:
time: 110 us; the launch traced here: 109 us
  blocking collectives  84.2 us (77%)
  starting transfers between devices  18.5 us (17%)
  Pallas kernels  3.48 us (3%)
    all_to_all x1, blocking collectives, sent_to_all(): lax.all_to_all(jnp.broadcast_to(x[None], (peers, *x.shape)), axis, 0, 0,...  28.3 us
    all_to_all x1, blocking collectives, per_device(): got = lax.all_to_all(sums.reshape(-1, *ROW_TILE), FAR, 0, 0, tiled=True)  19.1 us
    all_to_all x1, blocking collectives, per_device(): lax.all_to_all(every, OWNERS, 0, 0, tiled=True).reshape(zls, 1, features)  13.3 us
    all_to_all x1, blocking collectives, per_device(): got = lax.all_to_all(terms, NEAR, 0, 0, tiled=True)  12.7 us
    ppermute x1, starting transfers between devices, per_device(): got_tokens = lax.ppermute(tokens, 'c', swap)  12.6 us
    all_to_all x1, blocking collectives, per_device(): weights = lax.all_to_all(packed, 'x', 0, 0, tiled=True)  10.8 us
    ppermute x1, starting transfers between devices, per_device(): other = lax.ppermute(pre, 'c', swap)  5.99 us
    pallas_call x1, Pallas kernels, per_device(): pl.pallas_call(lambda *refs: pre_kernel(width, *refs), out_shape=(jax.Sha...  2.48 us
  transfers between devices with their start and end apart: 2, of which 1 were waited for; matrix products, arithmetic and copies ran while one was open for 1% of the time, Pallas kernels for 0%

profile of v4, /device:TPU:1, one launch (start us, length us, event | category | flops | bytes accessed | tf_op | source)
XLA Modules:
  0.0 109.3 jit_solution(8049875055247647627)
XLA Ops:
  0.6 0.0 copy-start
  0.6 12.6 %collective-permute-start = (bf16[128,8192]{1,0:T(8,128)(2,1)}, bf16[128,8192]{1,0:T(8,128)(2,1)}, u32[]{:S(2)}, u32[]{:S(2)}) collective-permute-start(bf16[128,8192]{1,0:T(8,128)(2,1)} %refs_1_.3), channel_id=1, source_target_pairs={{0,1},{1,0},{2,3},{3,2},{4,5},{5,4},{6,7},{7,6},{8,9},{9,8},{10,11... | collective-permute-start | bytes 6291464 | tf_op jit(solution)/shard_map/ppermute | solution.py:228
  13.2 0.8 fusion
  14.0 28.3 %all_to_all.25.refs_2_ = bf16[96,8,128]{2,1,0:T(8,128)(2,1)S(1)} all-to-all(bf16[96,8,128]{2,1,0:T(8,128)(2,1)S(1)} %broadcast_in_dim.8), channel_id=1, replica_groups=mesh['yh'=4,'yl'=2,'zh'=4,'x'=4,'zl'=3,'c'=2] {'zl','yl','yh','zh'}, dimensions={0} | all-to-all | bytes 393216 | tf_op jit(solution)/shard_map/all_to_all | solution.py:25
  42.3 0.3 pack.1
  42.6 10.8 %all_to_all.26.refs_3_ = bf16[4,33,16,128]{3,2,1,0:T(8,128)(2,1)S(1)} all-to-all(bf16[4,33,16,128]{3,2,1,0:T(8,128)(2,1)S(1)} %pack.1), channel_id=1, replica_groups=mesh['yh'=4,'yl'=2,'zh'=4,'x'=4,'zl'=3,'c'=2] {'x'}, dimensions={0} | all-to-all | bytes 1081344 | tf_op jit(solution)/shard_map/all_to_all | solution.py:241
  53.4 0.0 collective-permute-done.refs_2_
  53.4 0.0 copy-done
  53.4 2.5 %pre.1 = (f32[96,256]{1,0:T(8,128)S(1)}, bf16[128,4096]{1,0:T(8,128)(2,1)S(1)}) custom-call(s32[1]{0:T(128)} %bitcast.1.refs_0_, bf16[128,8192]{1,0:T(8,128)(2,1)S(1)} %copy-done, bf16[128,8192]{1,0:T(8,128)(2,1)} %collective-permute-done.refs_2_, bf16[4,33,16,128]{3,2,1,0:T(8,128)(2,1)S(1)} %all_to_all.26.refs_3_), custom_call_target="tpu_custom_call" | custom-call | tf_op jit(solution)/shard_map/pre/pallas_call | solution.py:244
  55.9 6.0 %collective-permute-start.1 = (f32[96,256]{1,0:T(8,128)S(1)}, f32[96,256]{1,0:T(8,128)S(1)}, u32[]{:S(2)}, u32[]{:S(2)}) collective-permute-start(f32[96,256]{1,0:T(8,128)S(1)} %get-tuple-element.6.refs_3_), channel_id=1, source_target_pairs={{0,1},{1,0},{2,3},{3,2},{4,5},{5,4},{6,7},{7,6},{8,9},{9,8},{10,11... | collective-permute-start | bytes 294920 | tf_op jit(solution)/shard_map/ppermute | solution.py:256
  61.9 0.9 collective-permute-done.1.refs_4_
  62.8 0.6 grad.1
  63.4 12.7 %all_to_all.27.refs_0_ = bf16[8,17,16,128]{3,2,1,0:T(8,128)(2,1)S(1)} all-to-all(bf16[8,17,16,128]{3,2,1,0:T(8,128)(2,1)S(1)} %grad.1), channel_id=1, replica_groups=mesh['yh'=4,'yl'=2,'zh'=4,'x'=4,'zl'=3,'c'=2] {'x','yl'}, dimensions={0} | all-to-all | bytes 1114112 | tf_op jit(solution)/shard_map/all_to_all | solution.py:268
  76.2 0.1 sums.1
  76.3 19.1 %all_to_all.28.refs_1_ = bf16[48,8,128]{2,1,0:T(8,128)(2,1)S(1)} all-to-all(bf16[48,8,128]{2,1,0:T(8,128)(2,1)S(1)} %bitcast.15), channel_id=1, replica_groups=mesh['yh'=4,'yl'=2,'zh'=4,'x'=4,'zl'=3,'c'=2] {'zl','yh','zh'}, dimensions={0} | all-to-all | bytes 196608 | tf_op jit(solution)/shard_map/all_to_all | solution.py:270
  95.4 0.1 final.1
  95.4 13.3 %all_to_all.29 = f32[24,8,128]{2,1,0:T(8,128)S(1)} all-to-all(f32[24,8,128]{2,1,0:T(8,128)S(1)} %final.1), channel_id=1, replica_groups=mesh['yh'=4,'yl'=2,'zh'=4,'x'=4,'zl'=3,'c'=2] {'zl','c','x'}, dimensions={0} | all-to-all | bytes 196608 | tf_op jit(solution)/shard_map/all_to_all | solution.py:280
  108.7 0.6 fusion.1
  (3 shorter events, 0.1 us)
Async XLA Ops:
  0.6 52.8 %copy-start = (bf16[128,8192]{1,0:T(8,128)(2,1)S(1)}, bf16[128,8192]{1,0:T(8,128)(2,1)}, u32[]{:S(2)}) copy-start(bf16[128,8192]{1,0:T(8,128)(2,1)} %refs_1_.3) | copy-start | bytes 6291460
  0.6 52.8 %collective-permute-start = (bf16[128,8192]{1,0:T(8,128)(2,1)}, bf16[128,8192]{1,0:T(8,128)(2,1)}, u32[]{:S(2)}, u32[]{:S(2)}) collective-permute-start(bf16[128,8192]{1,0:T(8,128)(2,1)} %refs_1_.3), channel_id=1, source_target_pairs={{0,1},{1,0},{2,3},{3,2},{4,5},{5,4},{6,7},{7,6},{8,9},{9,8},{10,11... | collective-permute-start | bytes 6291464 | tf_op jit(solution)/shard_map/ppermute | solution.py:228
  55.9 6.9 %collective-permute-start.1 = (f32[96,256]{1,0:T(8,128)S(1)}, f32[96,256]{1,0:T(8,128)S(1)}, u32[]{:S(2)}, u32[]{:S(2)}) collective-permute-start(f32[96,256]{1,0:T(8,128)S(1)} %get-tuple-element.6.refs_3_), channel_id=1, source_target_pairs={{0,1},{1,0},{2,3},{3,2},{4,5},{5,4},{6,7},{7,6},{8,9},{9,8},{10,11... | collective-permute-start | bytes 294920 | tf_op jit(solution)/shard_map/ppermute | solution.py:256

commit v5 on v4

--- a/solution.py
+++ b/solution.py
@@ -69,7 +69,7 @@
     )
 
 
-def pack_kernel(plane_ref, out_ref):
+def pack_kernel(plane_ref, unused_ref, out_ref):
     rows, width = plane_ref.shape
     two = 2 * rows // 3
     peers = out_ref.shape[0]
@@ -83,46 +83,32 @@
         out_ref[p, out_ref.shape[1] - 1] = square
 
 
-def own_columns(core, part, parts, width):
-    return pl.ds(pl.multiple_of((core * parts + part) * width, width), width)
-
-
-def pre_kernel(width, core_ref, tok_ref, got_ref, w_ref, out_ref, half_ref, sem):
+def token_columns(core, part, parts, width, tok_ref, got_ref):
+    columns = pl.ds(pl.multiple_of((core * parts + part) * width, width), width)
+    return jnp.concatenate([tok_ref[:, columns], got_ref[:, columns]], axis=0)
+
+
+def pre_kernel(width, core_ref, tok_ref, got_ref, w_ref, out_ref):
     parts, tiles = w_ref.shape[:2]
     two = (tiles - 1) * HIGH * LANES // width
     hid = two // 2
     core = core_ref[0]
-    side = half_ref.shape[1]
-    copy = pltpu.make_async_copy(
-        got_ref.at[:, pl.ds(pl.multiple_of(core * side, side), side)], half_ref, sem
-    )
-    copy.start()
-    weights = [from_tiles(w_ref, part, two, width) for part in range(parts)]
+    pre = jnp.zeros((2 * tok_ref.shape[0], two), F32)
     square = jnp.zeros((hid, hid), F32)
-    own = jnp.zeros((tok_ref.shape[0], two), F32)
     for part in range(parts):
-        own += lax.dot_general(
-            tok_ref[:, own_columns(core, part, parts, width)],
-            weights[part],
+        pre += lax.dot_general(
+            token_columns(core, part, parts, width, tok_ref, got_ref),
+            from_tiles(w_ref, part, two, width),
             NT,
             preferred_element_type=F32,
         )
         square += tile_to_square(w_ref[part, tiles - 1], hid, hid)
-    copy.wait()
-    other = jnp.zeros((tok_ref.shape[0], two), F32)
-    for part in range(parts):
-        other += lax.dot_general(
-            half_ref[:, part * width : (part + 1) * width],
-            weights[part],
-            NT,
-            preferred_element_type=F32,
-        )
-    out_ref[:two, :] = jnp.concatenate([own, other], axis=0).T
+    out_ref[:two, :] = pre.T
     blank = jnp.zeros((hid, out_ref.shape[1] - hid), F32)
     out_ref[two:, :] = jnp.concatenate([square, blank], axis=1)
 
 
-def grad_kernel(loss_scale, width, parts, core_ref, tok_ref, half_ref, own_ref, other_ref, out_ref):
+def grad_kernel(loss_scale, width, parts, core_ref, tok_ref, got_ref, own_ref, other_ref, out_ref):
     peers, tiles = out_ref.shape[:2]
     lanes = peers // parts
     hid = own_ref.shape[0] // 3
@@ -148,8 +134,7 @@
     square = lax.dot_general(hidden, hidden, NT, preferred_element_type=F32)
     squares = [square_to_tile(square[k * share : (k + 1) * share]) for k in range(lanes)]
     for part in range(parts):
-        own = tok_ref[:, own_columns(core, part, parts, width)]
-        chip = jnp.concatenate([own, half_ref[:, part * width : (part + 1) * width]], axis=0)
+        chip = token_columns(core, part, parts, width, tok_ref, got_ref)
         terms = jnp.dot(grads, chip, preferred_element_type=F32).astype(BF16)
         for lane in range(lanes):
             to = part * lanes + lane
@@ -231,28 +216,27 @@
     mine = lax.select_n(kind, gate_weight, up_weight, down_weight)
     piece = lax.dynamic_slice(mine, (0, at), (1, width)).reshape(ROW_TILE)
     gathered = sent_to_all(piece, PLANE)
-    packed = call(
+    packed = pl.pallas_call(
         pack_kernel,
-        "pack",
-        (xs, tiles + 1, HIGH, LANES),
-        BF16,
-        gathered.reshape(rows, width),
-    )
+        out_shape=jax.ShapeDtypeStruct((xs, tiles + 1, HIGH, LANES), BF16),
+        in_specs=[VMEM, pl.BlockSpec(memory_space=pl.ANY)],
+        out_specs=VMEM,
+        compiler_params=pltpu.CompilerParams(vmem_limit_bytes=32 << 20),
+        name="pack",
+    )(gathered.reshape(rows, width), got_tokens)
     weights = lax.all_to_all(packed, "x", 0, 0, tiled=True)
 
     which = core.reshape(1)
-    pre, half = pl.pallas_call(
+    pre = call(
         lambda *refs: pre_kernel(width, *refs),
-        out_shape=(
-            jax.ShapeDtypeStruct((rows, cs * tok_rows), F32),
-            jax.ShapeDtypeStruct((tok_rows, features // cs), BF16),
-        ),
-        in_specs=[SMEM, VMEM, pl.BlockSpec(memory_space=pl.ANY), VMEM],
-        out_specs=(VMEM, VMEM),
-        scratch_shapes=[pltpu.SemaphoreType.DMA],
-        compiler_params=pltpu.CompilerParams(vmem_limit_bytes=32 << 20),
-        name="pre",
-    )(which, tokens, got_tokens, weights)
+        "pre",
+        (rows, cs * tok_rows),
+        F32,
+        which,
+        tokens,
+        got_tokens,
+        weights,
+    )
     other = lax.ppermute(pre, "c", swap)
     terms = call(
         lambda *refs: grad_kernel(loss_scale, width, xs, *refs),
@@ -261,7 +245,7 @@
         BF16,
         which,
         tokens,
-        half,
+        got_tokens,
         pre,
         other,
     )

time: 110 us -> 108 us (0.982)
  Pallas kernels: 3.48 us -> 1.73 us
    pallas_call x1, Pallas kernels: 2.48 us -> 0.25 us  [per_device(): pl.pallas_call(pack_kernel, out_shape=jax.ShapeDtypeStruct((xs, tiles + 1...]
where the time goes in v5:
time: 108 us
  blocking collectives  84.3 us (78%)
  starting transfers between devices  18.4 us (17%)
  Pallas kernels  1.73 us (2%)
    all_to_all x1, blocking collectives, sent_to_all(): lax.all_to_all(jnp.broadcast_to(x[None], (peers, *x.shape)), axis, 0, 0,...  28.3 us
    all_to_all x1, blocking collectives, per_device(): got = lax.all_to_all(sums.reshape(-1, *ROW_TILE), FAR, 0, 0, tiled=True)  19.1 us
    all_to_all x1, blocking collectives, per_device(): lax.all_to_all(every, OWNERS, 0, 0, tiled=True).reshape(zls, 1, features)  13.3 us
    all_to_all x1, blocking collectives, per_device(): got = lax.all_to_all(terms, NEAR, 0, 0, tiled=True)  12.7 us
    ppermute x1, starting transfers between devices, per_device(): got_tokens = lax.ppermute(tokens, 'c', swap)  12.4 us
    all_to_all x1, blocking collectives, per_device(): weights = lax.all_to_all(packed, 'x', 0, 0, tiled=True)  11 us
    ppermute x1, starting transfers between devices, per_device(): other = lax.ppermute(pre, 'c', swap)  5.99 us
  transfers between devices with their start and end apart: 2, of which 1 were waited for; matrix products, arithmetic and copies ran while one was open for 1% of the time, Pallas kernels for 0%

profile of v5, /device:TPU:1, one launch (start us, length us, event | category | flops | bytes accessed | tf_op | source)
XLA Modules:
  0.0 107.6 jit_solution(5288193142260012289)
XLA Ops:
  0.6 12.4 %collective-permute-start = (bf16[128,8192]{1,0:T(8,128)(2,1)}, bf16[128,8192]{1,0:T(8,128)(2,1)S(1)}, u32[]{:S(2)}, u32[]{:S(2)}) collective-permute-start(bf16[128,8192]{1,0:T(8,128)(2,1)} %refs_1_.3), channel_id=1, source_target_pairs={{0,1},{1,0},{2,3},{3,2},{4,5},{5,4},{6,7},{7,6},{8,9},{9,8},{10,11... | collective-permute-start | bytes 6291464 | tf_op jit(solution)/shard_map/ppermute | solution.py:213
  13.1 0.8 fusion
  13.9 28.3 %all_to_all.25.refs_2_ = bf16[96,8,128]{2,1,0:T(8,128)(2,1)S(1)} all-to-all(bf16[96,8,128]{2,1,0:T(8,128)(2,1)S(1)} %broadcast_in_dim.8), channel_id=1, replica_groups=mesh['yh'=4,'yl'=2,'zh'=4,'x'=4,'zl'=3,'c'=2] {'zl','yl','yh','zh'}, dimensions={0} | all-to-all | bytes 393216 | tf_op jit(solution)/shard_map/all_to_all | solution.py:25
  42.1 0.0 copy-start
  42.2 0.0 collective-permute-done.unused_ref.refs_2_
  42.2 0.3 pack.1
  42.4 11.0 %all_to_all.26.refs_3_ = bf16[4,33,16,128]{3,2,1,0:T(8,128)(2,1)S(1)} all-to-all(bf16[4,33,16,128]{3,2,1,0:T(8,128)(2,1)S(1)} %pack.1), channel_id=1, replica_groups=mesh['yh'=4,'yl'=2,'zh'=4,'x'=4,'zl'=3,'c'=2] {'x'}, dimensions={0} | all-to-all | bytes 1081344 | tf_op jit(solution)/shard_map/all_to_all | solution.py:227
  53.4 0.0 copy-done
  53.4 0.7 pre.1.refs_3_
  54.1 6.0 %collective-permute-start.1 = (f32[96,256]{1,0:T(8,128)S(1)}, f32[96,256]{1,0:T(8,128)S(1)}, u32[]{:S(2)}, u32[]{:S(2)}) collective-permute-start(f32[96,256]{1,0:T(8,128)S(1)} %pre.1.refs_3_), channel_id=1, source_target_pairs={{0,1},{1,0},{2,3},{3,2},{4,5},{5,4},{6,7},{7,6},{8,9},{9,8},{10,11... | collective-permute-start | bytes 294920 | tf_op jit(solution)/shard_map/ppermute | solution.py:240
  60.1 0.9 collective-permute-done.1.refs_4_
  61.1 0.6 grad.1
  61.7 12.7 %all_to_all.27.refs_0_ = bf16[8,17,16,128]{3,2,1,0:T(8,128)(2,1)S(1)} all-to-all(bf16[8,17,16,128]{3,2,1,0:T(8,128)(2,1)S(1)} %grad.1), channel_id=1, replica_groups=mesh['yh'=4,'yl'=2,'zh'=4,'x'=4,'zl'=3,'c'=2] {'x','yl'}, dimensions={0} | all-to-all | bytes 1114112 | tf_op jit(solution)/shard_map/all_to_all | solution.py:252
  74.4 0.1 sums.1
  74.5 19.1 %all_to_all.28.refs_1_ = bf16[48,8,128]{2,1,0:T(8,128)(2,1)S(1)} all-to-all(bf16[48,8,128]{2,1,0:T(8,128)(2,1)S(1)} %bitcast.15), channel_id=1, replica_groups=mesh['yh'=4,'yl'=2,'zh'=4,'x'=4,'zl'=3,'c'=2] {'zl','yh','zh'}, dimensions={0} | all-to-all | bytes 196608 | tf_op jit(solution)/shard_map/all_to_all | solution.py:254
  93.6 0.1 final.1
  93.7 13.3 %all_to_all.29 = f32[24,8,128]{2,1,0:T(8,128)S(1)} all-to-all(f32[24,8,128]{2,1,0:T(8,128)S(1)} %final.1), channel_id=1, replica_groups=mesh['yh'=4,'yl'=2,'zh'=4,'x'=4,'zl'=3,'c'=2] {'zl','c','x'}, dimensions={0} | all-to-all | bytes 196608 | tf_op jit(solution)/shard_map/all_to_all | solution.py:264
  106.9 0.6 fusion.1
  (3 shorter events, 0.1 us)
Async XLA Ops:
  0.6 41.5 %collective-permute-start = (bf16[128,8192]{1,0:T(8,128)(2,1)}, bf16[128,8192]{1,0:T(8,128)(2,1)S(1)}, u32[]{:S(2)}, u32[]{:S(2)}) collective-permute-start(bf16[128,8192]{1,0:T(8,128)(2,1)} %refs_1_.3), channel_id=1, source_target_pairs={{0,1},{1,0},{2,3},{3,2},{4,5},{5,4},{6,7},{7,6},{8,9},{9,8},{10,11... | collective-permute-start | bytes 6291464 | tf_op jit(solution)/shard_map/ppermute | solution.py:213
  42.1 11.3 %copy-start = (bf16[128,8192]{1,0:T(8,128)(2,1)S(1)}, bf16[128,8192]{1,0:T(8,128)(2,1)}, u32[]{:S(2)}) copy-start(bf16[128,8192]{1,0:T(8,128)(2,1)} %refs_1_.3) | copy-start | bytes 6291460
  54.1 6.9 %collective-permute-start.1 = (f32[96,256]{1,0:T(8,128)S(1)}, f32[96,256]{1,0:T(8,128)S(1)}, u32[]{:S(2)}, u32[]{:S(2)}) collective-permute-start(f32[96,256]{1,0:T(8,128)S(1)} %pre.1.refs_3_), channel_id=1, source_target_pairs={{0,1},{1,0},{2,3},{3,2},{4,5},{5,4},{6,7},{7,6},{8,9},{9,8},{10,11... | collective-permute-start | bytes 294920 | tf_op jit(solution)/shard_map/ppermute | solution.py:240

commit v6 on v5

--- a/solution.py
+++ b/solution.py
@@ -8,9 +8,9 @@
 
 AXES = ("yh", "yl", "zh", "x", "zl", "c")
 BLK = AXES[:3]
-PLANE = ("zl", "yl", "yh", "zh")
+PLANE = ("yh", "yl", "zh", "zl")
 NEAR = ("x", "yl")
-FAR = ("zl", "yh", "zh")
+FAR = ("yh", "zh", "zl")
 OWNERS = ("zl", "c", "x")
 ROW_TILE = (8, 128)
 HIGH, LANES = 16, 128
@@ -215,7 +215,8 @@
     at = (core * xs + lax.axis_index("x")) * width
     mine = lax.select_n(kind, gate_weight, up_weight, down_weight)
     piece = lax.dynamic_slice(mine, (0, at), (1, width)).reshape(ROW_TILE)
-    gathered = sent_to_all(piece, PLANE)
+    by_place = sent_to_all(piece, PLANE).reshape(*(lax.axis_size(a) for a in PLANE), *ROW_TILE)
+    gathered = by_place.transpose(3, 1, 0, 2, 4, 5).reshape(rows, *ROW_TILE)
     packed = pl.pallas_call(
         pack_kernel,
         out_shape=jax.ShapeDtypeStruct((xs, tiles + 1, HIGH, LANES), BF16),
@@ -251,7 +252,8 @@
     )
     got = lax.all_to_all(terms, NEAR, 0, 0, tiled=True)
     sums = call(lambda *refs: sum_kernel(hid, *refs), "sums", (rows // yls, width), BF16, got)
-    got = lax.all_to_all(sums.reshape(-1, *ROW_TILE), FAR, 0, 0, tiled=True)
+    by_kind = sums.reshape(zls, -1, *ROW_TILE).transpose(1, 0, 2, 3).reshape(-1, *ROW_TILE)
+    got = lax.all_to_all(by_kind, FAR, 0, 0, tiled=True)
     every = call(
         lambda *refs: final_kernel(loss_scale, *refs),
         "final",

time: 108 us -> 108 us (level)
  no operation moved by 1% of the time
where the time goes in v6:
time: 108 us
  blocking collectives  84.5 us (78%)
  starting transfers between devices  18.5 us (17%)
  Pallas kernels  1.73 us (2%)
    all_to_all x1, blocking collectives, sent_to_all(): lax.all_to_all(jnp.broadcast_to(x[None], (peers, *x.shape)), axis, 0, 0,...  27.6 us
    all_to_all x1, blocking collectives, per_device(): got = lax.all_to_all(by_kind, FAR, 0, 0, tiled=True)  19.7 us
    all_to_all x1, blocking collectives, per_device(): lax.all_to_all(every, OWNERS, 0, 0, tiled=True).reshape(zls, 1, features)  13.3 us
    all_to_all x1, blocking collectives, per_device(): got = lax.all_to_all(terms, NEAR, 0, 0, tiled=True)  12.9 us
    ppermute x1, starting transfers between devices, per_device(): got_tokens = lax.ppermute(tokens, 'c', swap)  12.4 us
    all_to_all x1, blocking collectives, per_device(): weights = lax.all_to_all(packed, 'x', 0, 0, tiled=True)  11 us
    ppermute x1, starting transfers between devices, per_device(): other = lax.ppermute(pre, 'c', swap)  6.1 us
  transfers between devices with their start and end apart: 2, of which 1 were waited for; matrix products, arithmetic and copies ran while one was open for 1% of the time, Pallas kernels for 0%

profile of v6, /device:TPU:1, one launch (start us, length us, event | category | flops | bytes accessed | tf_op | source)
XLA Modules:
  0.0 107.9 jit_solution(3456450229378614513)
XLA Ops:
  0.6 12.4 %collective-permute-start = (bf16[128,8192]{1,0:T(8,128)(2,1)}, bf16[128,8192]{1,0:T(8,128)(2,1)S(1)}, u32[]{:S(2)}, u32[]{:S(2)}) collective-permute-start(bf16[128,8192]{1,0:T(8,128)(2,1)} %refs_1_.3), channel_id=1, source_target_pairs={{0,1},{1,0},{2,3},{3,2},{4,5},{5,4},{6,7},{7,6},{8,9},{9,8},{10,11... | collective-permute-start | bytes 6291464 | tf_op jit(solution)/shard_map/ppermute | solution.py:213
  13.1 0.8 fusion
  13.9 27.6 %all_to_all.25 = bf16[96,8,128]{2,1,0:T(8,128)(2,1)S(1)} all-to-all(bf16[96,8,128]{2,1,0:T(8,128)(2,1)S(1)} %broadcast_in_dim.8), channel_id=1, replica_groups=mesh['yh'=4,'yl'=2,'zh'=4,'x'=4,'zl'=3,'c'=2] {'yh','yl','zh','zl'}, dimensions={0} | all-to-all | bytes 393216 | tf_op jit(solution)/shard_map/all_to_all | solution.py:25
  41.6 0.0 copy-start
  41.6 0.0 collective-permute-done.unused_ref.refs_2_
  41.6 0.3 pack.1
  41.9 11.0 %all_to_all.26.refs_3_ = bf16[4,33,16,128]{3,2,1,0:T(8,128)(2,1)S(1)} all-to-all(bf16[4,33,16,128]{3,2,1,0:T(8,128)(2,1)S(1)} %pack.1), channel_id=1, replica_groups=mesh['yh'=4,'yl'=2,'zh'=4,'x'=4,'zl'=3,'c'=2] {'x'}, dimensions={0} | all-to-all | bytes 1081344 | tf_op jit(solution)/shard_map/all_to_all | solution.py:228
  52.8 0.0 copy-done
  52.8 0.7 pre.1.refs_3_
  53.6 6.1 %collective-permute-start.1 = (f32[96,256]{1,0:T(8,128)S(1)}, f32[96,256]{1,0:T(8,128)S(1)}, u32[]{:S(2)}, u32[]{:S(2)}) collective-permute-start(f32[96,256]{1,0:T(8,128)S(1)} %pre.1.refs_3_), channel_id=1, source_target_pairs={{0,1},{1,0},{2,3},{3,2},{4,5},{5,4},{6,7},{7,6},{8,9},{9,8},{10,11... | collective-permute-start | bytes 294920 | tf_op jit(solution)/shard_map/ppermute | solution.py:241
  59.7 0.9 collective-permute-done.1.refs_4_
  60.6 0.6 grad.1
  61.2 12.9 %all_to_all.27.refs_0_ = bf16[8,17,16,128]{3,2,1,0:T(8,128)(2,1)S(1)} all-to-all(bf16[8,17,16,128]{3,2,1,0:T(8,128)(2,1)S(1)} %grad.1), channel_id=1, replica_groups=mesh['yh'=4,'yl'=2,'zh'=4,'x'=4,'zl'=3,'c'=2] {'x','yl'}, dimensions={0} | all-to-all | bytes 1114112 | tf_op jit(solution)/shard_map/all_to_all | solution.py:253
  74.1 0.1 sums.1
  74.2 19.7 %all_to_all.28.refs_1_ = bf16[48,8,128]{2,1,0:T(8,128)(2,1)S(1)} all-to-all(bf16[48,8,128]{2,1,0:T(8,128)(2,1)S(1)} %bitcast.27), channel_id=1, replica_groups=mesh['yh'=4,'yl'=2,'zh'=4,'x'=4,'zl'=3,'c'=2] {'yh','zh','zl'}, dimensions={0} | all-to-all | bytes 196608 | tf_op jit(solution)/shard_map/all_to_all | solution.py:256
  93.9 0.1 final.1
  94.0 13.3 %all_to_all.29 = f32[24,8,128]{2,1,0:T(8,128)S(1)} all-to-all(f32[24,8,128]{2,1,0:T(8,128)S(1)} %final.1), channel_id=1, replica_groups=mesh['yh'=4,'yl'=2,'zh'=4,'x'=4,'zl'=3,'c'=2] {'zl','c','x'}, dimensions={0} | all-to-all | bytes 196608 | tf_op jit(solution)/shard_map/all_to_all | solution.py:266
  107.3 0.6 fusion.1
  (5 shorter events, 0.1 us)
Async XLA Ops:
  0.6 41.0 %collective-permute-start = (bf16[128,8192]{1,0:T(8,128)(2,1)}, bf16[128,8192]{1,0:T(8,128)(2,1)S(1)}, u32[]{:S(2)}, u32[]{:S(2)}) collective-permute-start(bf16[128,8192]{1,0:T(8,128)(2,1)} %refs_1_.3), channel_id=1, source_target_pairs={{0,1},{1,0},{2,3},{3,2},{4,5},{5,4},{6,7},{7,6},{8,9},{9,8},{10,11... | collective-permute-start | bytes 6291464 | tf_op jit(solution)/shard_map/ppermute | solution.py:213
  41.6 11.3 %copy-start = (bf16[128,8192]{1,0:T(8,128)(2,1)S(1)}, bf16[128,8192]{1,0:T(8,128)(2,1)}, u32[]{:S(2)}) copy-start(bf16[128,8192]{1,0:T(8,128)(2,1)} %refs_1_.3) | copy-start | bytes 6291460
  53.6 7.0 %collective-permute-start.1 = (f32[96,256]{1,0:T(8,128)S(1)}, f32[96,256]{1,0:T(8,128)S(1)}, u32[]{:S(2)}, u32[]{:S(2)}) collective-permute-start(f32[96,256]{1,0:T(8,128)S(1)} %pre.1.refs_3_), channel_id=1, source_target_pairs={{0,1},{1,0},{2,3},{3,2},{4,5},{5,4},{6,7},{7,6},{8,9},{9,8},{10,11... | collective-permute-start | bytes 294920 | tf_op jit(solution)/shard_map/ppermute | solution.py:241

commit v7 on v5

--- a/solution.py
+++ b/solution.py
@@ -8,7 +8,7 @@
 
 AXES = ("yh", "yl", "zh", "x", "zl", "c")
 BLK = AXES[:3]
-PLANE = ("zl", "yl", "yh", "zh")
+PLANE = ("yl", "yh", "zh")
 NEAR = ("x", "yl")
 FAR = ("zl", "yh", "zh")
 OWNERS = ("zl", "c", "x")
@@ -213,9 +213,12 @@
     got_tokens = lax.ppermute(tokens, "c", swap)
 
     at = (core * xs + lax.axis_index("x")) * width
-    mine = lax.select_n(kind, gate_weight, up_weight, down_weight)
-    piece = lax.dynamic_slice(mine, (0, at), (1, width)).reshape(ROW_TILE)
-    gathered = sent_to_all(piece, PLANE)
+    pieces = [
+        lax.dynamic_slice(weight, (0, at), (1, width)).reshape(ROW_TILE)
+        for weight in (gate_weight, up_weight, down_weight)
+    ]
+    by_place = sent_to_all(jnp.concatenate(pieces, axis=0), PLANE)
+    gathered = by_place.reshape(hid, 3, *ROW_TILE).transpose(1, 0, 2, 3).reshape(rows, *ROW_TILE)
     packed = pl.pallas_call(
         pack_kernel,
         out_shape=jax.ShapeDtypeStruct((xs, tiles + 1, HIGH, LANES), BF16),

time: 108 us -> 108 us (level)
  blocking collectives: 84.3 us -> 62.3 us
  waiting for transfers between devices: 0.92 us -> 14.9 us
  starting transfers between devices: 18.4 us -> 25.4 us
  local copies, waits for them, and re-layouts: 0.72 us -> 2.16 us
    all_to_all x1 -> x0, blocking collectives: 19.1 us -> none  [per_device(): got = lax.all_to_all(sums.reshape(-1, *ROW_TILE), FAR, 0, 0, tiled=True)]
    all_to_all x0 -> x1, waiting for transfers between devices: none -> 13.9 us  [per_device(): got = lax.all_to_all(sums.reshape(-1, *ROW_TILE), FAR, 0, 0, tiled=True)]
    all_to_all x0 -> x1, starting transfers between devices: none -> 8.19 us  [per_device(): got = lax.all_to_all(sums.reshape(-1, *ROW_TILE), FAR, 0, 0, tiled=True)]
    all_to_all x1, blocking collectives: 28.3 us -> 24.7 us  [sent_to_all(): lax.all_to_all(jnp.broadcast_to(x[None], (peers, *x.shape)), axis, 0, 0,...]
    ppermute x1, starting transfers between devices: 5.99 us -> 4.77 us  [per_device(): other = lax.ppermute(pre, 'c', swap)]
  transfers between devices with their start and end apart: 2 -> 3, of which waited for: 1 -> 2; matrix products, arithmetic and copies ran while one was open for 1% -> 1% of each run, Pallas kernels for 0% -> 0%
where the time goes in v7:
time: 108 us; the launch traced here: 107 us
  blocking collectives  62.3 us (58%)
  starting transfers between devices  25.4 us (24%)
  waiting for transfers between devices  14.9 us (14%)
  local copies, waits for them, and re-layouts  2.16 us (2%)
  Pallas kernels  1.73 us (2%)
    all_to_all x1, blocking collectives, sent_to_all(): lax.all_to_all(jnp.broadcast_to(x[None], (peers, *x.shape)), axis, 0, 0,...  24.7 us
    all_to_all x1, waiting for transfers between devices, per_device(): got = lax.all_to_all(sums.reshape(-1, *ROW_TILE), FAR, 0, 0, tiled=True)  13.9 us
    all_to_all x1, blocking collectives, per_device(): lax.all_to_all(every, OWNERS, 0, 0, tiled=True).reshape(zls, 1, features)  13.2 us
    all_to_all x1, blocking collectives, per_device(): got = lax.all_to_all(terms, NEAR, 0, 0, tiled=True)  12.7 us
    ppermute x1, starting transfers between devices, per_device(): got_tokens = lax.ppermute(tokens, 'c', swap)  12.4 us
    all_to_all x1, blocking collectives, per_device(): weights = lax.all_to_all(packed, 'x', 0, 0, tiled=True)  11.7 us
    all_to_all x1, starting transfers between devices, per_device(): got = lax.all_to_all(sums.reshape(-1, *ROW_TILE), FAR, 0, 0, tiled=True)  8.19 us
    ppermute x1, starting transfers between devices, per_device(): other = lax.ppermute(pre, 'c', swap)  4.77 us
  transfers between devices with their start and end apart: 3, of which 2 were waited for; matrix products, arithmetic and copies ran while one was open for 1% of the time, Pallas kernels for 0%

profile of v7, /device:TPU:1, one launch (start us, length us, event | category | flops | bytes accessed | tf_op | source)
XLA Modules:
  0.0 107.2 jit_solution(15220327678408677425)
XLA Ops:
  0.6 0.0 copy-start
  0.6 12.4 %collective-permute-start = (bf16[128,8192]{1,0:T(8,128)(2,1)}, bf16[128,8192]{1,0:T(8,128)(2,1)S(1)}, u32[]{:S(2)}, u32[]{:S(2)}) collective-permute-start(bf16[128,8192]{1,0:T(8,128)(2,1)} %refs_1_.3), channel_id=1, source_target_pairs={{0,1},{1,0},{2,3},{3,2},{4,5},{5,4},{6,7},{7,6},{8,9},{9,8},{10,11... | collective-permute-start | bytes 6291464 | tf_op jit(solution)/shard_map/ppermute | solution.py:213
  13.1 0.0 copy-done
  13.1 0.7 dynamic-slice_reduce_fusion
  13.9 24.7 %all_to_all.25 = bf16[32,24,128]{2,1,0:T(8,128)(2,1)S(1)} all-to-all(bf16[32,24,128]{2,1,0:T(8,128)(2,1)S(1)} %broadcast_in_dim.2), channel_id=1, replica_groups=mesh['yh'=4,'yl'=2,'zh'=4,'x'=4,'zl'=3,'c'=2] {'yl','yh','zh'}, dimensions={0} | all-to-all | bytes 393216 | tf_op jit(solution)/shard_map/all_to_all | solution.py:25
  38.7 0.0 copy-start.1
  38.7 0.0 collective-permute-done.unused_ref.refs_2_
  38.7 0.3 pack.1
  39.0 11.7 %all_to_all.26.refs_3_ = bf16[4,33,16,128]{3,2,1,0:T(8,128)(2,1)S(1)} all-to-all(bf16[4,33,16,128]{3,2,1,0:T(8,128)(2,1)S(1)} %pack.1), channel_id=1, replica_groups=mesh['yh'=4,'yl'=2,'zh'=4,'x'=4,'zl'=3,'c'=2] {'x'}, dimensions={0} | all-to-all | bytes 1081344 | tf_op jit(solution)/shard_map/all_to_all | solution.py:230
  50.7 0.0 copy-done.1
  50.7 0.7 pre.1.refs_3_
  51.4 4.8 %collective-permute-start.1 = (f32[96,256]{1,0:T(8,128)S(1)}, f32[96,256]{1,0:T(8,128)S(1)}, u32[]{:S(2)}, u32[]{:S(2)}) collective-permute-start(f32[96,256]{1,0:T(8,128)S(1)} %pre.1.refs_3_), channel_id=1, source_target_pairs={{0,1},{1,0},{2,3},{3,2},{4,5},{5,4},{6,7},{7,6},{8,9},{9,8},{10,11... | collective-permute-start | bytes 294920 | tf_op jit(solution)/shard_map/ppermute | solution.py:243
  56.2 0.9 collective-permute-done.1.refs_4_
  57.1 0.6 grad.1
  57.7 12.7 %all_to_all.27.refs_0_ = bf16[8,17,16,128]{3,2,1,0:T(8,128)(2,1)S(1)} all-to-all(bf16[8,17,16,128]{3,2,1,0:T(8,128)(2,1)S(1)} %grad.1), channel_id=1, replica_groups=mesh['yh'=4,'yl'=2,'zh'=4,'x'=4,'zl'=3,'c'=2] {'x','yl'}, dimensions={0} | all-to-all | bytes 1114112 | tf_op jit(solution)/shard_map/all_to_all | solution.py:255
  70.4 0.1 sums.1
  70.5 0.6 copy.10
  71.1 8.2 %all-to-all-start.3 = ((bf16[48,8,128]{2,1,0:T(8,128)(2,1)}), bf16[48,8,128]{2,1,0:T(8,128)(2,1)S(1)}, u32[]{:S(2)}, u32[]{:S(2)}) async-start(bf16[48,8,128]{2,1,0:T(8,128)(2,1)} %bitcast.16), calls=%async_computation.3 | async-start | bytes 196608 | tf_op jit(solution)/shard_map/all_to_all | solution.py:257
  79.3 13.9 %all-to-all-done.3.refs_1_ = bf16[48,8,128]{2,1,0:T(8,128)(2,1)S(1)} async-done(((bf16[48,8,128]{2,1,0:T(8,128)(2,1)}), bf16[48,8,128]{2,1,0:T(8,128)(2,1)S(1)}, u32[]{:S(2)}, u32[]{:S(2)}) %all-to-all-start.3) | async-done | bytes 98336 | tf_op jit(solution)/shard_map/all_to_all | solution.py:257
  93.3 0.1 final.1
  93.3 13.2 %all_to_all.28 = f32[24,8,128]{2,1,0:T(8,128)S(1)} all-to-all(f32[24,8,128]{2,1,0:T(8,128)S(1)} %final.1), channel_id=1, replica_groups=mesh['yh'=4,'yl'=2,'zh'=4,'x'=4,'zl'=3,'c'=2] {'zl','c','x'}, dimensions={0} | all-to-all | bytes 196608 | tf_op jit(solution)/shard_map/all_to_all | solution.py:267
  106.6 0.6 fusion
  (5 shorter events, 0.1 us)
Async XLA Ops:
  0.6 12.5 %copy-start = (bf16[1,8192]{1,0:T(2,128)(2,1)S(1)}, bf16[1,8192]{1,0:T(2,128)(2,1)}, u32[]{:S(2)}) copy-start(bf16[1,8192]{1,0:T(2,128)(2,1)} %param.5) | copy-start | bytes 49156
  0.6 38.1 %collective-permute-start = (bf16[128,8192]{1,0:T(8,128)(2,1)}, bf16[128,8192]{1,0:T(8,128)(2,1)S(1)}, u32[]{:S(2)}, u32[]{:S(2)}) collective-permute-start(bf16[128,8192]{1,0:T(8,128)(2,1)} %refs_1_.3), channel_id=1, source_target_pairs={{0,1},{1,0},{2,3},{3,2},{4,5},{5,4},{6,7},{7,6},{8,9},{9,8},{10,11... | collective-permute-start | bytes 6291464 | tf_op jit(solution)/shard_map/ppermute | solution.py:213
  38.7 12.0 %copy-start.1 = (bf16[128,8192]{1,0:T(8,128)(2,1)S(1)}, bf16[128,8192]{1,0:T(8,128)(2,1)}, u32[]{:S(2)}) copy-start(bf16[128,8192]{1,0:T(8,128)(2,1)} %refs_1_.3) | copy-start | bytes 6291460
  51.4 5.7 %collective-permute-start.1 = (f32[96,256]{1,0:T(8,128)S(1)}, f32[96,256]{1,0:T(8,128)S(1)}, u32[]{:S(2)}, u32[]{:S(2)}) collective-permute-start(f32[96,256]{1,0:T(8,128)S(1)} %pre.1.refs_3_), channel_id=1, source_target_pairs={{0,1},{1,0},{2,3},{3,2},{4,5},{5,4},{6,7},{7,6},{8,9},{9,8},{10,11... | collective-permute-start | bytes 294920 | tf_op jit(solution)/shard_map/ppermute | solution.py:243
  71.1 22.1 %all-to-all-start.3 = ((bf16[48,8,128]{2,1,0:T(8,128)(2,1)}), bf16[48,8,128]{2,1,0:T(8,128)(2,1)S(1)}, u32[]{:S(2)}, u32[]{:S(2)}) async-start(bf16[48,8,128]{2,1,0:T(8,128)(2,1)} %bitcast.16), calls=%async_computation.3 | async-start | bytes 196608 | tf_op jit(solution)/shard_map/all_to_all | solution.py:257

commit v8 on v7

--- a/solution.py
+++ b/solution.py
@@ -207,12 +207,13 @@
     rows = 3 * hid
     tiles = 2 * hid * width // (HIGH * LANES)
     core = lax.axis_index("c")
-    kind = lax.axis_index("zl")
+    kind = lax.axis_index("zl").reshape(1)
     swap = [(i, (i + 1) % cs) for i in range(cs)]
 
     got_tokens = lax.ppermute(tokens, "c", swap)
 
     at = (core * xs + lax.axis_index("x")) * width
+    at, kind = lax.optimization_barrier((at, kind))
     pieces = [
         lax.dynamic_slice(weight, (0, at), (1, width)).reshape(ROW_TILE)
         for weight in (gate_weight, up_weight, down_weight)
@@ -260,7 +261,7 @@
         "final",
         (xs * zls * cs, *ROW_TILE),
         F32,
-        kind.reshape(1),
+        kind,
         got,
         gathered,
     )

time: 108 us -> 107 us (level)
  blocking collectives: 62.3 us -> 84.3 us
  waiting for transfers between devices: 14.9 us -> 0.92 us
  starting transfers between devices: 25.4 us -> 17.2 us
    all_to_all x0 -> x1, blocking collectives: none -> 22 us  [per_device(): got = lax.all_to_all(sums.reshape(-1, *ROW_TILE), FAR, 0, 0, tiled=True)]
    all_to_all x1 -> x0, waiting for transfers between devices: 13.9 us -> none  [per_device(): got = lax.all_to_all(sums.reshape(-1, *ROW_TILE), FAR, 0, 0, tiled=True)]
    all_to_all x1 -> x0, starting transfers between devices: 8.19 us -> none  [per_device(): got = lax.all_to_all(sums.reshape(-1, *ROW_TILE), FAR, 0, 0, tiled=True)]
  transfers between devices with their start and end apart: 3 -> 2, of which waited for: 2 -> 1; matrix products, arithmetic and copies ran while one was open for 1% -> 1% of each run, Pallas kernels for 0% -> 0%
where the time goes in v8:
time: 107 us
  blocking collectives  84.3 us (79%)
  starting transfers between devices  17.2 us (16%)
  Pallas kernels  1.73 us (2%)
  local copies, waits for them, and re-layouts  1.68 us (2%)
    all_to_all x1, blocking collectives, sent_to_all(): lax.all_to_all(jnp.broadcast_to(x[None], (peers, *x.shape)), axis, 0, 0,...  24.7 us
    all_to_all x1, blocking collectives, per_device(): got = lax.all_to_all(sums.reshape(-1, *ROW_TILE), FAR, 0, 0, tiled=True)  22 us
    all_to_all x1, blocking collectives, per_device(): lax.all_to_all(every, OWNERS, 0, 0, tiled=True).reshape(zls, 1, features)  13.2 us
    all_to_all x1, blocking collectives, per_device(): got = lax.all_to_all(terms, NEAR, 0, 0, tiled=True)  12.7 us
    ppermute x1, starting transfers between devices, per_device(): got_tokens = lax.ppermute(tokens, 'c', swap)  12.4 us
    all_to_all x1, blocking collectives, per_device(): weights = lax.all_to_all(packed, 'x', 0, 0, tiled=True)  11.7 us
    ppermute x1, starting transfers between devices, per_device(): other = lax.ppermute(pre, 'c', swap)  4.77 us
  transfers between devices with their start and end apart: 2, of which 1 were waited for; matrix products, arithmetic and copies ran while one was open for 1% of the time, Pallas kernels for 0%

profile of v8, /device:TPU:1, one launch (start us, length us, event | category | flops | bytes accessed | tf_op | source)
XLA Modules:
  0.0 106.6 jit_solution(2926330906407195707)
XLA Ops:
  0.6 0.0 copy-start
  0.6 12.4 %collective-permute-start = (bf16[128,8192]{1,0:T(8,128)(2,1)}, bf16[128,8192]{1,0:T(8,128)(2,1)S(1)}, u32[]{:S(2)}, u32[]{:S(2)}) collective-permute-start(bf16[128,8192]{1,0:T(8,128)(2,1)} %refs_1_.3), channel_id=1, source_target_pairs={{0,1},{1,0},{2,3},{3,2},{4,5},{5,4},{6,7},{7,6},{8,9},{9,8},{10,11... | collective-permute-start | bytes 6291464 | tf_op jit(solution)/shard_map/ppermute | solution.py:213
  13.1 0.0 copy-done
  13.1 0.1 dynamic-slice_reduce_fusion.2
  13.2 0.8 dynamic-slice_reduce_fusion
  14.1 24.7 %all_to_all.25 = bf16[32,24,128]{2,1,0:T(8,128)(2,1)S(1)} all-to-all(bf16[32,24,128]{2,1,0:T(8,128)(2,1)S(1)} %broadcast_in_dim.2), channel_id=1, replica_groups=mesh['yh'=4,'yl'=2,'zh'=4,'x'=4,'zl'=3,'c'=2] {'yl','yh','zh'}, dimensions={0} | all-to-all | bytes 393216 | tf_op jit(solution)/shard_map/all_to_all | solution.py:25
  38.8 0.0 copy-start.1
  38.9 0.0 collective-permute-done.unused_ref.refs_2_
  38.9 0.3 pack.1
  39.1 11.7 %all_to_all.26.refs_3_ = bf16[4,33,16,128]{3,2,1,0:T(8,128)(2,1)S(1)} all-to-all(bf16[4,33,16,128]{3,2,1,0:T(8,128)(2,1)S(1)} %pack.1), channel_id=1, replica_groups=mesh['yh'=4,'yl'=2,'zh'=4,'x'=4,'zl'=3,'c'=2] {'x'}, dimensions={0} | all-to-all | bytes 1081344 | tf_op jit(solution)/shard_map/all_to_all | solution.py:231
  50.8 0.0 copy-done.1
  50.8 0.7 pre.1.refs_3_
  51.5 4.8 %collective-permute-start.1 = (f32[96,256]{1,0:T(8,128)S(1)}, f32[96,256]{1,0:T(8,128)S(1)}, u32[]{:S(2)}, u32[]{:S(2)}) collective-permute-start(f32[96,256]{1,0:T(8,128)S(1)} %pre.1.refs_3_), channel_id=1, source_target_pairs={{0,1},{1,0},{2,3},{3,2},{4,5},{5,4},{6,7},{7,6},{8,9},{9,8},{10,11... | collective-permute-start | bytes 294920 | tf_op jit(solution)/shard_map/ppermute | solution.py:244
  56.3 0.9 collective-permute-done.1.refs_4_
  57.2 0.6 grad.1
  57.9 12.7 %all_to_all.27.refs_0_ = bf16[8,17,16,128]{3,2,1,0:T(8,128)(2,1)S(1)} all-to-all(bf16[8,17,16,128]{3,2,1,0:T(8,128)(2,1)S(1)} %grad.1), channel_id=1, replica_groups=mesh['yh'=4,'yl'=2,'zh'=4,'x'=4,'zl'=3,'c'=2] {'x','yl'}, dimensions={0} | all-to-all | bytes 1114112 | tf_op jit(solution)/shard_map/all_to_all | solution.py:256
  70.5 0.1 sums.1
  70.7 22.0 %all_to_all.28.refs_1_ = bf16[48,8,128]{2,1,0:T(8,128)(2,1)S(1)} all-to-all(bf16[48,8,128]{2,1,0:T(8,128)(2,1)S(1)} %bitcast.24), channel_id=1, replica_groups=mesh['yh'=4,'yl'=2,'zh'=4,'x'=4,'zl'=3,'c'=2] {'zl','yh','zh'}, dimensions={0} | all-to-all | bytes 196608 | tf_op jit(solution)/shard_map/all_to_all | solution.py:258
  92.6 0.1 final.1
  92.7 13.2 %all_to_all.29 = f32[24,8,128]{2,1,0:T(8,128)S(1)} all-to-all(f32[24,8,128]{2,1,0:T(8,128)S(1)} %final.1), channel_id=1, replica_groups=mesh['yh'=4,'yl'=2,'zh'=4,'x'=4,'zl'=3,'c'=2] {'zl','c','x'}, dimensions={0} | all-to-all | bytes 196608 | tf_op jit(solution)/shard_map/all_to_all | solution.py:268
  105.9 0.6 fusion
  (5 shorter events, 0.1 us)
Async XLA Ops:
  0.6 12.5 %copy-start = (bf16[1,8192]{1,0:T(2,128)(2,1)S(1)}, bf16[1,8192]{1,0:T(2,128)(2,1)}, u32[]{:S(2)}) copy-start(bf16[1,8192]{1,0:T(2,128)(2,1)} %param.5) | copy-start | bytes 49156
  0.6 38.2 %collective-permute-start = (bf16[128,8192]{1,0:T(8,128)(2,1)}, bf16[128,8192]{1,0:T(8,128)(2,1)S(1)}, u32[]{:S(2)}, u32[]{:S(2)}) collective-permute-start(bf16[128,8192]{1,0:T(8,128)(2,1)} %refs_1_.3), channel_id=1, source_target_pairs={{0,1},{1,0},{2,3},{3,2},{4,5},{5,4},{6,7},{7,6},{8,9},{9,8},{10,11... | collective-permute-start | bytes 6291464 | tf_op jit(solution)/shard_map/ppermute | solution.py:213
  38.8 12.0 %copy-start.1 = (bf16[128,8192]{1,0:T(8,128)(2,1)S(1)}, bf16[128,8192]{1,0:T(8,128)(2,1)}, u32[]{:S(2)}) copy-start(bf16[128,8192]{1,0:T(8,128)(2,1)} %refs_1_.3) | copy-start | bytes 6291460
  51.5 5.7 %collective-permute-start.1 = (f32[96,256]{1,0:T(8,128)S(1)}, f32[96,256]{1,0:T(8,128)S(1)}, u32[]{:S(2)}, u32[]{:S(2)}) collective-permute-start(f32[96,256]{1,0:T(8,128)S(1)} %pre.1.refs_3_), channel_id=1, source_target_pairs={{0,1},{1,0},{2,3},{3,2},{4,5},{5,4},{6,7},{7,6},{8,9},{9,8},{10,11... | collective-permute-start | bytes 294920 | tf_op jit(solution)/shard_map/ppermute | solution.py:244

commit v9 on v8

--- a/solution.py
+++ b/solution.py
@@ -69,7 +69,7 @@
     )
 
 
-def pack_kernel(plane_ref, unused_ref, out_ref):
+def pack_kernel(plane_ref, out_ref):
     rows, width = plane_ref.shape
     two = 2 * rows // 3
     peers = out_ref.shape[0]
@@ -210,8 +210,6 @@
     kind = lax.axis_index("zl").reshape(1)
     swap = [(i, (i + 1) % cs) for i in range(cs)]
 
-    got_tokens = lax.ppermute(tokens, "c", swap)
-
     at = (core * xs + lax.axis_index("x")) * width
     at, kind = lax.optimization_barrier((at, kind))
     pieces = [
@@ -219,15 +217,16 @@
         for weight in (gate_weight, up_weight, down_weight)
     ]
     by_place = sent_to_all(jnp.concatenate(pieces, axis=0), PLANE)
+    by_place, tokens = lax.optimization_barrier((by_place, tokens))
+    got_tokens = lax.ppermute(tokens, "c", swap)
     gathered = by_place.reshape(hid, 3, *ROW_TILE).transpose(1, 0, 2, 3).reshape(rows, *ROW_TILE)
-    packed = pl.pallas_call(
+    packed = call(
         pack_kernel,
-        out_shape=jax.ShapeDtypeStruct((xs, tiles + 1, HIGH, LANES), BF16),
-        in_specs=[VMEM, pl.BlockSpec(memory_space=pl.ANY)],
-        out_specs=VMEM,
-        compiler_params=pltpu.CompilerParams(vmem_limit_bytes=32 << 20),
-        name="pack",
-    )(gathered.reshape(rows, width), got_tokens)
+        "pack",
+        (xs, tiles + 1, HIGH, LANES),
+        BF16,
+        gathered.reshape(rows, width),
+    )
     weights = lax.all_to_all(packed, "x", 0, 0, tiled=True)
 
     which = core.reshape(1)

time: 107 us -> 108 us (level)
  starting transfers between devices: 17.2 us -> 7.05 us
  blocking collectives: 84.3 us -> 94.4 us
    all_to_all x1, blocking collectives: 24.7 us -> 34.5 us  [sent_to_all(): lax.all_to_all(jnp.broadcast_to(x[None], (peers, *x.shape)), axis, 0, 0,...]
    ppermute x1, starting transfers between devices: 12.4 us -> 3.88 us  [per_device(): got_tokens = lax.ppermute(tokens, 'c', swap)]
    ppermute x1, starting transfers between devices: 4.77 us -> 3.18 us  [per_device(): other = lax.ppermute(pre, 'c', swap)]
    all_to_all x1, blocking collectives: 11.7 us -> 13.2 us  [per_device(): weights = lax.all_to_all(packed, 'x', 0, 0, tiled=True)]
    all_to_all x1, blocking collectives: 22 us -> 20.8 us  [per_device(): got = lax.all_to_all(sums.reshape(-1, *ROW_TILE), FAR, 0, 0, tiled=True)]
  transfers between devices with their start and end apart: 2 -> 2, of which waited for: 1 -> 1; matrix products, arithmetic and copies ran while one was open for 1% -> 0% of each run, Pallas kernels for 0% -> 0%
where the time goes in v9:
time: 108 us; the launch traced here: 107 us
  blocking collectives  94.4 us (87%)
  starting transfers between devices  7.05 us (7%)
  local copies, waits for them, and re-layouts  2.39 us (2%)
  Pallas kernels  1.75 us (2%)
    all_to_all x1, blocking collectives, sent_to_all(): lax.all_to_all(jnp.broadcast_to(x[None], (peers, *x.shape)), axis, 0, 0,...  34.5 us
    all_to_all x1, blocking collectives, per_device(): got = lax.all_to_all(sums.reshape(-1, *ROW_TILE), FAR, 0, 0, tiled=True)  20.8 us
    all_to_all x1, blocking collectives, per_device(): lax.all_to_all(every, OWNERS, 0, 0, tiled=True).reshape(zls, 1, features)  13.2 us
    all_to_all x1, blocking collectives, per_device(): weights = lax.all_to_all(packed, 'x', 0, 0, tiled=True)  13.2 us
    all_to_all x1, blocking collectives, per_device(): got = lax.all_to_all(terms, NEAR, 0, 0, tiled=True)  12.7 us
    ppermute x1, starting transfers between devices, per_device(): got_tokens = lax.ppermute(tokens, 'c', swap)  3.88 us
    ppermute x1, starting transfers between devices, per_device(): other = lax.ppermute(pre, 'c', swap)  3.18 us
  transfers between devices with their start and end apart: 2, of which 1 were waited for; matrix products, arithmetic and copies ran while one was open for 0% of the time, Pallas kernels for 0%

profile of v9, /device:TPU:1, one launch (start us, length us, event | category | flops | bytes accessed | tf_op | source)
XLA Modules:
  0.0 107.2 jit_solution(8937832709272980370)
XLA Ops:
  0.6 0.0 copy-start
  0.6 0.0 copy-start.1
  0.7 0.7 copy-done
  1.4 0.1 dynamic-slice_reduce_fusion.2
  1.5 0.8 dynamic-slice_reduce_fusion
  2.4 34.5 %all_to_all.25 = bf16[32,24,128]{2,1,0:T(8,128)(2,1)S(1)} all-to-all(bf16[32,24,128]{2,1,0:T(8,128)(2,1)S(1)} %broadcast_in_dim.2), channel_id=1, replica_groups=mesh['yh'=4,'yl'=2,'zh'=4,'x'=4,'zl'=3,'c'=2] {'yl','yh','zh'}, dimensions={0} | all-to-all | bytes 393216 | tf_op jit(solution)/shard_map/all_to_all | solution.py:25
  36.9 3.9 %collective-permute-start = (bf16[128,8192]{1,0:T(8,128)(2,1)}, bf16[128,8192]{1,0:T(8,128)(2,1)S(1)}, u32[]{:S(2)}, u32[]{:S(2)}) collective-permute-start(bf16[128,8192]{1,0:T(8,128)(2,1)} %refs_1_.1), channel_id=1, source_target_pairs={{0,1},{1,0},{2,3},{3,2},{4,5},{5,4},{6,7},{7,6},{8,9},{9,8},{10,11... | collective-permute-start | bytes 6291464 | tf_op jit(solution)/shard_map/ppermute | solution.py:221
  40.8 0.3 pack.1
  41.1 13.2 %all_to_all.26.refs_3_ = bf16[4,33,16,128]{3,2,1,0:T(8,128)(2,1)S(1)} all-to-all(bf16[4,33,16,128]{3,2,1,0:T(8,128)(2,1)S(1)} %pack.1), channel_id=1, replica_groups=mesh['yh'=4,'yl'=2,'zh'=4,'x'=4,'zl'=3,'c'=2] {'x'}, dimensions={0} | all-to-all | bytes 1081344 | tf_op jit(solution)/shard_map/all_to_all | solution.py:230
  54.2 0.0 collective-permute-done.refs_2_
  54.2 0.0 copy-done.1
  54.2 0.8 pre.1.refs_3_
  55.0 3.2 %collective-permute-start.1 = (f32[96,256]{1,0:T(8,128)S(1)}, f32[96,256]{1,0:T(8,128)S(1)}, u32[]{:S(2)}, u32[]{:S(2)}) collective-permute-start(f32[96,256]{1,0:T(8,128)S(1)} %pre.1.refs_3_), channel_id=1, source_target_pairs={{0,1},{1,0},{2,3},{3,2},{4,5},{5,4},{6,7},{7,6},{8,9},{9,8},{10,11... | collective-permute-start | bytes 294920 | tf_op jit(solution)/shard_map/ppermute | solution.py:243
  58.2 0.9 collective-permute-done.1.refs_4_
  59.1 0.6 grad.1
  59.7 12.7 %all_to_all.27.refs_0_ = bf16[8,17,16,128]{3,2,1,0:T(8,128)(2,1)S(1)} all-to-all(bf16[8,17,16,128]{3,2,1,0:T(8,128)(2,1)S(1)} %grad.1), channel_id=1, replica_groups=mesh['yh'=4,'yl'=2,'zh'=4,'x'=4,'zl'=3,'c'=2] {'x','yl'}, dimensions={0} | all-to-all | bytes 1114112 | tf_op jit(solution)/shard_map/all_to_all | solution.py:255
  72.4 0.1 sums.1
  72.5 20.8 %all_to_all.28.refs_1_ = bf16[48,8,128]{2,1,0:T(8,128)(2,1)S(1)} all-to-all(bf16[48,8,128]{2,1,0:T(8,128)(2,1)S(1)} %bitcast.24), channel_id=1, replica_groups=mesh['yh'=4,'yl'=2,'zh'=4,'x'=4,'zl'=3,'c'=2] {'zl','yh','zh'}, dimensions={0} | all-to-all | bytes 196608 | tf_op jit(solution)/shard_map/all_to_all | solution.py:257
  93.3 0.1 final.1
  93.4 13.2 %all_to_all.29 = f32[24,8,128]{2,1,0:T(8,128)S(1)} all-to-all(f32[24,8,128]{2,1,0:T(8,128)S(1)} %final.1), channel_id=1, replica_groups=mesh['yh'=4,'yl'=2,'zh'=4,'x'=4,'zl'=3,'c'=2] {'zl','c','x'}, dimensions={0} | all-to-all | bytes 196608 | tf_op jit(solution)/shard_map/all_to_all | solution.py:267
  106.6 0.6 fusion
  (5 shorter events, 0.1 us)
Async XLA Ops:
  0.6 0.8 copy-start
  0.6 53.6 %copy-start.1 = (bf16[128,8192]{1,0:T(8,128)(2,1)S(1)}, bf16[128,8192]{1,0:T(8,128)(2,1)}, u32[]{:S(2)}) copy-start(bf16[128,8192]{1,0:T(8,128)(2,1)} %refs_1_.1) | copy-start | bytes 6291460
  36.9 17.4 %collective-permute-start = (bf16[128,8192]{1,0:T(8,128)(2,1)}, bf16[128,8192]{1,0:T(8,128)(2,1)S(1)}, u32[]{:S(2)}, u32[]{:S(2)}) collective-permute-start(bf16[128,8192]{1,0:T(8,128)(2,1)} %refs_1_.1), channel_id=1, source_target_pairs={{0,1},{1,0},{2,3},{3,2},{4,5},{5,4},{6,7},{7,6},{8,9},{9,8},{10,11... | collective-permute-start | bytes 6291464 | tf_op jit(solution)/shard_map/ppermute | solution.py:221
  55.0 4.1 %collective-permute-start.1 = (f32[96,256]{1,0:T(8,128)S(1)}, f32[96,256]{1,0:T(8,128)S(1)}, u32[]{:S(2)}, u32[]{:S(2)}) collective-permute-start(f32[96,256]{1,0:T(8,128)S(1)} %pre.1.refs_3_), channel_id=1, source_target_pairs={{0,1},{1,0},{2,3},{3,2},{4,5},{5,4},{6,7},{7,6},{8,9},{9,8},{10,11... | collective-permute-start | bytes 294920 | tf_op jit(solution)/shard_map/ppermute | solution.py:243

commit v10 on v8

--- a/solution.py
+++ b/solution.py
@@ -93,17 +93,17 @@
     two = (tiles - 1) * HIGH * LANES // width
     hid = two // 2
     core = core_ref[0]
-    pre = jnp.zeros((2 * tok_ref.shape[0], two), F32)
+    pre = jnp.zeros((two, 2 * tok_ref.shape[0]), F32)
     square = jnp.zeros((hid, hid), F32)
     for part in range(parts):
         pre += lax.dot_general(
+            from_tiles(w_ref, part, two, width),
             token_columns(core, part, parts, width, tok_ref, got_ref),
-            from_tiles(w_ref, part, two, width),
             NT,
             preferred_element_type=F32,
         )
         square += tile_to_square(w_ref[part, tiles - 1], hid, hid)
-    out_ref[:two, :] = pre.T
+    out_ref[:two, :] = pre
     blank = jnp.zeros((hid, out_ref.shape[1] - hid), F32)
     out_ref[two:, :] = jnp.concatenate([square, blank], axis=1)
 

time: 107 us -> 107 us (level)
  no operation moved by 1% of the time
where the time goes in v10:
time: 107 us
  blocking collectives  84.3 us (79%)
  starting transfers between devices  17.2 us (16%)
  Pallas kernels  1.75 us (2%)
  local copies, waits for them, and re-layouts  1.68 us (2%)
    all_to_all x1, blocking collectives, sent_to_all(): lax.all_to_all(jnp.broadcast_to(x[None], (peers, *x.shape)), axis, 0, 0,...  24.7 us
    all_to_all x1, blocking collectives, per_device(): got = lax.all_to_all(sums.reshape(-1, *ROW_TILE), FAR, 0, 0, tiled=True)  22 us
    all_to_all x1, blocking collectives, per_device(): lax.all_to_all(every, OWNERS, 0, 0, tiled=True).reshape(zls, 1, features)  13.2 us
    all_to_all x1, blocking collectives, per_device(): got = lax.all_to_all(terms, NEAR, 0, 0, tiled=True)  12.7 us
    ppermute x1, starting transfers between devices, per_device(): got_tokens = lax.ppermute(tokens, 'c', swap)  12.4 us
    all_to_all x1, blocking collectives, per_device(): weights = lax.all_to_all(packed, 'x', 0, 0, tiled=True)  11.7 us
    ppermute x1, starting transfers between devices, per_device(): other = lax.ppermute(pre, 'c', swap)  4.77 us
  transfers between devices with their start and end apart: 2, of which 1 were waited for; matrix products, arithmetic and copies ran while one was open for 1% of the time, Pallas kernels for 0%

profile of v10, /device:TPU:1, one launch (start us, length us, event | category | flops | bytes accessed | tf_op | source)
XLA Modules:
  0.0 106.6 jit_solution(11242372226026843571)
XLA Ops:
  0.6 0.0 copy-start
  0.6 12.4 %collective-permute-start = (bf16[128,8192]{1,0:T(8,128)(2,1)}, bf16[128,8192]{1,0:T(8,128)(2,1)S(1)}, u32[]{:S(2)}, u32[]{:S(2)}) collective-permute-start(bf16[128,8192]{1,0:T(8,128)(2,1)} %refs_1_.3), channel_id=1, source_target_pairs={{0,1},{1,0},{2,3},{3,2},{4,5},{5,4},{6,7},{7,6},{8,9},{9,8},{10,11... | collective-permute-start | bytes 6291464 | tf_op jit(solution)/shard_map/ppermute | solution.py:213
  13.1 0.0 copy-done
  13.1 0.1 dynamic-slice_reduce_fusion.2
  13.2 0.8 dynamic-slice_reduce_fusion
  14.1 24.7 %all_to_all.25 = bf16[32,24,128]{2,1,0:T(8,128)(2,1)S(1)} all-to-all(bf16[32,24,128]{2,1,0:T(8,128)(2,1)S(1)} %broadcast_in_dim.2), channel_id=1, replica_groups=mesh['yh'=4,'yl'=2,'zh'=4,'x'=4,'zl'=3,'c'=2] {'yl','yh','zh'}, dimensions={0} | all-to-all | bytes 393216 | tf_op jit(solution)/shard_map/all_to_all | solution.py:25
  38.8 0.0 copy-start.1
  38.9 0.0 collective-permute-done.unused_ref.refs_2_
  38.9 0.3 pack.1
  39.1 11.7 %all_to_all.26.refs_3_ = bf16[4,33,16,128]{3,2,1,0:T(8,128)(2,1)S(1)} all-to-all(bf16[4,33,16,128]{3,2,1,0:T(8,128)(2,1)S(1)} %pack.1), channel_id=1, replica_groups=mesh['yh'=4,'yl'=2,'zh'=4,'x'=4,'zl'=3,'c'=2] {'x'}, dimensions={0} | all-to-all | bytes 1081344 | tf_op jit(solution)/shard_map/all_to_all | solution.py:231
  50.8 0.0 copy-done.1
  50.8 0.8 pre.1.refs_3_
  51.6 4.8 %collective-permute-start.1 = (f32[96,256]{1,0:T(8,128)S(1)}, f32[96,256]{1,0:T(8,128)S(1)}, u32[]{:S(2)}, u32[]{:S(2)}) collective-permute-start(f32[96,256]{1,0:T(8,128)S(1)} %pre.1.refs_3_), channel_id=1, source_target_pairs={{0,1},{1,0},{2,3},{3,2},{4,5},{5,4},{6,7},{7,6},{8,9},{9,8},{10,11... | collective-permute-start | bytes 294920 | tf_op jit(solution)/shard_map/ppermute | solution.py:244
  56.4 0.9 collective-permute-done.1.refs_4_
  57.3 0.6 grad.1
  57.9 12.7 %all_to_all.27.refs_0_ = bf16[8,17,16,128]{3,2,1,0:T(8,128)(2,1)S(1)} all-to-all(bf16[8,17,16,128]{3,2,1,0:T(8,128)(2,1)S(1)} %grad.1), channel_id=1, replica_groups=mesh['yh'=4,'yl'=2,'zh'=4,'x'=4,'zl'=3,'c'=2] {'x','yl'}, dimensions={0} | all-to-all | bytes 1114112 | tf_op jit(solution)/shard_map/all_to_all | solution.py:256
  70.6 0.1 sums.1
  70.7 22.0 %all_to_all.28.refs_1_ = bf16[48,8,128]{2,1,0:T(8,128)(2,1)S(1)} all-to-all(bf16[48,8,128]{2,1,0:T(8,128)(2,1)S(1)} %bitcast.24), channel_id=1, replica_groups=mesh['yh'=4,'yl'=2,'zh'=4,'x'=4,'zl'=3,'c'=2] {'zl','yh','zh'}, dimensions={0} | all-to-all | bytes 196608 | tf_op jit(solution)/shard_map/all_to_all | solution.py:258
  92.6 0.1 final.1
  92.7 13.2 %all_to_all.29 = f32[24,8,128]{2,1,0:T(8,128)S(1)} all-to-all(f32[24,8,128]{2,1,0:T(8,128)S(1)} %final.1), channel_id=1, replica_groups=mesh['yh'=4,'yl'=2,'zh'=4,'x'=4,'zl'=3,'c'=2] {'zl','c','x'}, dimensions={0} | all-to-all | bytes 196608 | tf_op jit(solution)/shard_map/all_to_all | solution.py:268
  105.9 0.6 fusion
  (5 shorter events, 0.1 us)
Async XLA Ops:
  0.6 12.5 %copy-start = (bf16[1,8192]{1,0:T(2,128)(2,1)S(1)}, bf16[1,8192]{1,0:T(2,128)(2,1)}, u32[]{:S(2)}) copy-start(bf16[1,8192]{1,0:T(2,128)(2,1)} %param.5) | copy-start | bytes 49156
  0.6 38.2 %collective-permute-start = (bf16[128,8192]{1,0:T(8,128)(2,1)}, bf16[128,8192]{1,0:T(8,128)(2,1)S(1)}, u32[]{:S(2)}, u32[]{:S(2)}) collective-permute-start(bf16[128,8192]{1,0:T(8,128)(2,1)} %refs_1_.3), channel_id=1, source_target_pairs={{0,1},{1,0},{2,3},{3,2},{4,5},{5,4},{6,7},{7,6},{8,9},{9,8},{10,11... | collective-permute-start | bytes 6291464 | tf_op jit(solution)/shard_map/ppermute | solution.py:213
  38.8 12.0 %copy-start.1 = (bf16[128,8192]{1,0:T(8,128)(2,1)S(1)}, bf16[128,8192]{1,0:T(8,128)(2,1)}, u32[]{:S(2)}) copy-start(bf16[128,8192]{1,0:T(8,128)(2,1)} %refs_1_.3) | copy-start | bytes 6291460
  51.6 5.7 %collective-permute-start.1 = (f32[96,256]{1,0:T(8,128)S(1)}, f32[96,256]{1,0:T(8,128)S(1)}, u32[]{:S(2)}, u32[]{:S(2)}) collective-permute-start(f32[96,256]{1,0:T(8,128)S(1)} %pre.1.refs_3_), channel_id=1, source_target_pairs={{0,1},{1,0},{2,3},{3,2},{4,5},{5,4},{6,7},{7,6},{8,9},{9,8},{10,11... | collective-permute-start | bytes 294920 | tf_op jit(solution)/shard_map/ppermute | solution.py:244

commit v11 on v10

--- a/solution.py
+++ b/solution.py
@@ -187,6 +187,19 @@
             out_ref[to] = result
 
 
+def out_kernel(every_ref, *refs):
+    outs, sems = refs[:3], refs[3]
+    share = every_ref.shape[0] // 3
+    copies = [
+        pltpu.make_async_copy(every_ref.at[pl.ds(kind * share, share)], out, sems.at[kind])
+        for kind, out in enumerate(outs)
+    ]
+    for copy in copies:
+        copy.start()
+    for copy in copies:
+        copy.wait()
+
+
 def call(kernel, name, shape, dtype, *args):
     return pl.pallas_call(
         kernel,
@@ -265,8 +278,18 @@
         got,
         gathered,
     )
-    result = lax.all_to_all(every, OWNERS, 0, 0, tiled=True).reshape(zls, 1, features)
-    return (result[0], result[1], result[2])
+    result = lax.all_to_all(every, OWNERS, 0, 0, tiled=True)
+    one = jax.ShapeDtypeStruct((xs * cs, *ROW_TILE), F32)
+    outs = pl.pallas_call(
+        out_kernel,
+        out_shape=(one, one, one),
+        in_specs=[VMEM],
+        out_specs=(pl.BlockSpec(memory_space=pl.ANY),) * 3,
+        scratch_shapes=[pltpu.SemaphoreType.DMA((3,))],
+        compiler_params=pltpu.CompilerParams(vmem_limit_bytes=32 << 20),
+        name="out",
+    )(result)
+    return tuple(out.reshape(1, features) for out in outs)
 
 
 def solution(mesh):

time: 107 us -> 107 us (level)
  no operation moved by 1% of the time
where the time goes in v11:
time: 107 us
  blocking collectives  84.3 us (79%)
  starting transfers between devices  17.2 us (16%)
  Pallas kernels  2.42 us (2%)
    all_to_all x1, blocking collectives, sent_to_all(): lax.all_to_all(jnp.broadcast_to(x[None], (peers, *x.shape)), axis, 0, 0,...  24.7 us
    all_to_all x1, blocking collectives, per_device(): got = lax.all_to_all(sums.reshape(-1, *ROW_TILE), FAR, 0, 0, tiled=True)  22 us
    all_to_all x1, blocking collectives, per_device(): result = lax.all_to_all(every, OWNERS, 0, 0, tiled=True)  13.2 us
    all_to_all x1, blocking collectives, per_device(): got = lax.all_to_all(terms, NEAR, 0, 0, tiled=True)  12.7 us
    ppermute x1, starting transfers between devices, per_device(): got_tokens = lax.ppermute(tokens, 'c', swap)  12.4 us
    all_to_all x1, blocking collectives, per_device(): weights = lax.all_to_all(packed, 'x', 0, 0, tiled=True)  11.7 us
    ppermute x1, starting transfers between devices, per_device(): other = lax.ppermute(pre, 'c', swap)  4.77 us
  transfers between devices with their start and end apart: 2, of which 1 were waited for; matrix products, arithmetic and copies ran while one was open for 1% of the time, Pallas kernels for 0%

profile of v11, /device:TPU:1, one launch (start us, length us, event | category | flops | bytes accessed | tf_op | source)
XLA Modules:
  0.0 106.6 jit_solution(8908518870654598379)
XLA Ops:
  0.6 0.0 copy-start
  0.6 12.4 %collective-permute-start = (bf16[128,8192]{1,0:T(8,128)(2,1)}, bf16[128,8192]{1,0:T(8,128)(2,1)S(1)}, u32[]{:S(2)}, u32[]{:S(2)}) collective-permute-start(bf16[128,8192]{1,0:T(8,128)(2,1)} %refs_1_.3), channel_id=1, source_target_pairs={{0,1},{1,0},{2,3},{3,2},{4,5},{5,4},{6,7},{7,6},{8,9},{9,8},{10,11... | collective-permute-start | bytes 6291464 | tf_op jit(solution)/shard_map/ppermute | solution.py:226
  13.1 0.0 copy-done
  13.1 0.1 dynamic-slice_reduce_fusion.2
  13.2 0.8 dynamic-slice_reduce_fusion
  14.1 24.7 %all_to_all.25 = bf16[32,24,128]{2,1,0:T(8,128)(2,1)S(1)} all-to-all(bf16[32,24,128]{2,1,0:T(8,128)(2,1)S(1)} %broadcast_in_dim.2), channel_id=1, replica_groups=mesh['yh'=4,'yl'=2,'zh'=4,'x'=4,'zl'=3,'c'=2] {'yl','yh','zh'}, dimensions={0} | all-to-all | bytes 393216 | tf_op jit(solution)/shard_map/all_to_all | solution.py:25
  38.8 0.0 copy-start.1
  38.9 0.0 collective-permute-done.unused_ref.refs_2_
  38.9 0.3 pack.1
  39.1 11.7 %all_to_all.26.refs_3_ = bf16[4,33,16,128]{3,2,1,0:T(8,128)(2,1)S(1)} all-to-all(bf16[4,33,16,128]{3,2,1,0:T(8,128)(2,1)S(1)} %pack.1), channel_id=1, replica_groups=mesh['yh'=4,'yl'=2,'zh'=4,'x'=4,'zl'=3,'c'=2] {'x'}, dimensions={0} | all-to-all | bytes 1081344 | tf_op jit(solution)/shard_map/all_to_all | solution.py:244
  50.8 0.0 copy-done.1
  50.8 0.8 pre.1.refs_3_
  51.6 4.8 %collective-permute-start.1 = (f32[96,256]{1,0:T(8,128)S(1)}, f32[96,256]{1,0:T(8,128)S(1)}, u32[]{:S(2)}, u32[]{:S(2)}) collective-permute-start(f32[96,256]{1,0:T(8,128)S(1)} %pre.1.refs_3_), channel_id=1, source_target_pairs={{0,1},{1,0},{2,3},{3,2},{4,5},{5,4},{6,7},{7,6},{8,9},{9,8},{10,11... | collective-permute-start | bytes 294920 | tf_op jit(solution)/shard_map/ppermute | solution.py:257
  56.4 0.9 collective-permute-done.1.refs_4_
  57.3 0.6 grad.1
  57.9 12.7 %all_to_all.27.refs_0_ = bf16[8,17,16,128]{3,2,1,0:T(8,128)(2,1)S(1)} all-to-all(bf16[8,17,16,128]{3,2,1,0:T(8,128)(2,1)S(1)} %grad.1), channel_id=1, replica_groups=mesh['yh'=4,'yl'=2,'zh'=4,'x'=4,'zl'=3,'c'=2] {'x','yl'}, dimensions={0} | all-to-all | bytes 1114112 | tf_op jit(solution)/shard_map/all_to_all | solution.py:269
  70.6 0.1 sums.1
  70.7 22.0 %all_to_all.28.refs_1_ = bf16[48,8,128]{2,1,0:T(8,128)(2,1)S(1)} all-to-all(bf16[48,8,128]{2,1,0:T(8,128)(2,1)S(1)} %bitcast.24), channel_id=1, replica_groups=mesh['yh'=4,'yl'=2,'zh'=4,'x'=4,'zl'=3,'c'=2] {'zl','yh','zh'}, dimensions={0} | all-to-all | bytes 196608 | tf_op jit(solution)/shard_map/all_to_all | solution.py:271
  92.6 0.1 final.1
  92.7 13.2 %all_to_all.29.every_ref = f32[24,8,128]{2,1,0:T(8,128)S(1)} all-to-all(f32[24,8,128]{2,1,0:T(8,128)S(1)} %final.1), channel_id=1, replica_groups=mesh['yh'=4,'yl'=2,'zh'=4,'x'=4,'zl'=3,'c'=2] {'zl','c','x'}, dimensions={0} | all-to-all | bytes 196608 | tf_op jit(solution)/shard_map/all_to_all | solution.py:281
  105.9 0.7 out.1
  (5 shorter events, 0.1 us)
Async XLA Ops:
  0.6 12.5 %copy-start = (bf16[1,8192]{1,0:T(2,128)(2,1)S(1)}, bf16[1,8192]{1,0:T(2,128)(2,1)}, u32[]{:S(2)}) copy-start(bf16[1,8192]{1,0:T(2,128)(2,1)} %param.5) | copy-start | bytes 49156
  0.6 38.2 %collective-permute-start = (bf16[128,8192]{1,0:T(8,128)(2,1)}, bf16[128,8192]{1,0:T(8,128)(2,1)S(1)}, u32[]{:S(2)}, u32[]{:S(2)}) collective-permute-start(bf16[128,8192]{1,0:T(8,128)(2,1)} %refs_1_.3), channel_id=1, source_target_pairs={{0,1},{1,0},{2,3},{3,2},{4,5},{5,4},{6,7},{7,6},{8,9},{9,8},{10,11... | collective-permute-start | bytes 6291464 | tf_op jit(solution)/shard_map/ppermute | solution.py:226
  38.8 12.0 %copy-start.1 = (bf16[128,8192]{1,0:T(8,128)(2,1)S(1)}, bf16[128,8192]{1,0:T(8,128)(2,1)}, u32[]{:S(2)}) copy-start(bf16[128,8192]{1,0:T(8,128)(2,1)} %refs_1_.3) | copy-start | bytes 6291460
  51.6 5.7 %collective-permute-start.1 = (f32[96,256]{1,0:T(8,128)S(1)}, f32[96,256]{1,0:T(8,128)S(1)}, u32[]{:S(2)}, u32[]{:S(2)}) collective-permute-start(f32[96,256]{1,0:T(8,128)S(1)} %pre.1.refs_3_), channel_id=1, source_target_pairs={{0,1},{1,0},{2,3},{3,2},{4,5},{5,4},{6,7},{7,6},{8,9},{9,8},{10,11... | collective-permute-start | bytes 294920 | tf_op jit(solution)/shard_map/ppermute | solution.py:257
